TPU v7x, 32 devices: a whole 2x2x4 slice. The times are simulated.
32 devices in a mesh: expert: 4 (over x, core), fsdp: 8 (over z, y).
Axes of the slice: x: 2, y: 2, z: 4, core: 2. Of those that a mesh axis runs over, the one named last changes fastest.
Arguments:
- tokens: bfloat16 [4096, 1536], P(('expert', 'fsdp')), may hold values from -6 to 6
- gate_probs: float32 [4096, 2], P(('expert', 'fsdp')), may hold values from 0.1 to 1
- expert_ids: int32 [4096, 2], P(('expert', 'fsdp')), may hold values from 0 to 3, all different within a row; in each aligned block of 128 rows (0 to 127, 128 to 255, ...) at most 64 rows name the same one
- cotangent: bfloat16 [4096, 1536], P(('expert', 'fsdp')), may hold values from -0.59765625 to 0.59765625
- gate_weight: bfloat16 [4, 1536, 2048], P('expert', None, 'fsdp'), may hold values from -0.15625 to 0.15625
- up_weight: bfloat16 [4, 1536, 2048], P('expert', None, 'fsdp'), may hold values from -0.15625 to 0.15625
- down_weight: bfloat16 [4, 2048, 1536], P('expert', 'fsdp'), may hold values from -0.125 to 0.125
Outputs:
- mixed: bfloat16 [4096, 1536], P(('expert', 'fsdp'))
- d_tokens: bfloat16 [4096, 1536], P(('expert', 'fsdp'))
- d_gates: float32 [4096, 2], P(('expert', 'fsdp'))
- d_gate_weight: float32 [4, 1536, 2048], P('expert', None, 'fsdp')
- d_up_weight: float32 [4, 1536, 2048], P('expert', None, 'fsdp')
- d_down_weight: float32 [4, 2048, 1536], P('expert', 'fsdp')
Inputs may be any that keep to these rules, and one draw needn't show every extreme that they name: `expert_ids`: the two experts of a token differ. In the 128 rows of one device every expert is named exactly 64 times.
All inputs are finite; a program needn't handle non-finite values.
Results may differ from a plain program's by a relative error of at most 0.015.
Values may be sent and summed in bfloat16 or wider, within the bound.
No kernel may reach another device: no remote copies, remote signals or barrier semaphores. Data moves between devices by JAX's collectives and lax.ppermute only.
A program may use at most 192 MiB of HBM per device.

v0:
```python
import functools

import jax
import jax.numpy as jnp
from jax import lax
from jax.experimental import pallas as pl
from jax.experimental.pallas import tpu as pltpu
from jax.sharding import PartitionSpec as P

F32, BF16 = jnp.float32, jnp.bfloat16
CONTRACT_COLS = (((1,), (1,)), ((), ()))
ROUTE_ROWS = 8
VMEM_LIMIT = 24 * 1024 * 1024
BLOCK_VMEM = 56 * 1024 * 1024
SMALL_COST = pl.CostEstimate(flops=1000, bytes_accessed=1000, transcendentals=0)
ANY = pl.BlockSpec(memory_space=pl.ANY)
VMEM = pl.BlockSpec(memory_space=pltpu.VMEM)


def hop(value, axis, step):
    return lax.ppermute(value, axis, [(i, i ^ step) for i in range(lax.axis_size(axis))])


def inner_size(size):
    inner = 1
    while inner * inner * 4 <= size:
        inner *= 2
    return inner


def after(value, *earlier):
    return lax.optimization_barrier((value,) + earlier)[0]


def nt(a, b):
    return lax.dot_general(a, b, CONTRACT_COLS, preferred_element_type=F32)


def nn(a, b):
    return jnp.dot(a, b, preferred_element_type=F32)


def block_kernel(steps, packs, rows, places, has_acc, with_t, aliased, me_ref, *refs):
    refs = list(refs)
    take = lambda n: [refs.pop(0) for _ in range(n)]
    shards = len(places)
    pays = []
    for pack, ref in zip(packs, take(len(packs))):
        pays += [ref] if pack is None else [ref.at[i] for i in pack]
    weights = [take(2) for _ in steps]
    accs = take(shards) if has_acc else []
    take(aliased)
    outs = take(shards)
    (act_all,) = take(1)
    t_all = take(2) if with_t else []
    x_ref, c_ref, gu_ref, down_ref, dgu_ref, hp_ref = take(6)
    t_refs = take(2) if with_t else []
    acc_refs = take(shards) if has_acc else []
    w_sem, act_sem, t_sem, acc_sem = take(4)
    columns = x_ref.shape[1]
    width = hp_ref.shape[1] // len(steps)
    at = lambda n: slice(n * width, (n + 1) * width)
    w_copies = []
    for i, (gu, down) in enumerate(weights):
        targets = (gu_ref.at[:, at(2 * i)], gu_ref.at[:, at(2 * i + 1)], down_ref.at[:, at(i)])
        w_copies.append(
            [
                pltpu.make_async_copy(w, target, w_sem.at[i, m])
                for m, (w, target) in enumerate(zip((gu.at[0], gu.at[1], down), targets))
            ]
        )
    acc_copies = [
        pltpu.make_async_copy(a, r, acc_sem.at[j]) for j, (a, r) in enumerate(zip(accs, acc_refs))
    ]
    for copy in [c for group in w_copies for c in group] + acc_copies:
        copy.start()
    for j, pay in enumerate(pays):
        x_ref[j * rows : (j + 1) * rows, :] = pay[0:rows, :]
        c_ref[j * rows : (j + 1) * rows, :] = pay[rows : 2 * rows, :]
    t_copies = []
    if with_t:
        for n, source in enumerate((x_ref, c_ref)):
            t_refs[n][...] = source[...].T
            for j, place in enumerate(places):
                t_copies.append(
                    pltpu.make_async_copy(
                        t_refs[n].at[:, j * rows : (j + 1) * rows],
                        t_all[n].at[:, place : place + rows],
                        t_sem.at[n, j],
                    )
                )
        for copy in t_copies:
            copy.start()
    eye = (
        lax.broadcasted_iota(jnp.int32, (rows, rows), 0)
        == lax.broadcasted_iota(jnp.int32, (rows, rows), 1)
    ).astype(BF16)
    routes = [pay[2 * rows : 2 * rows + ROUTE_ROWS, 0:rows] for pay in pays]
    stand = jnp.concatenate([nt(eye, route) for route in routes], axis=0)
    lying = jnp.concatenate([route.astype(F32) for route in routes], axis=1)
    gates = [jnp.zeros((1, shards * rows), F32), jnp.zeros((1, shards * rows), F32)]
    act_copies = []
    for i, step in enumerate(steps):
        e = (me_ref[0] ^ step).astype(F32)
        prob = jnp.where(stand[:, 4:5] == e, stand[:, 0:1] + stand[:, 2:3], 0.0)
        prob = prob + jnp.where(stand[:, 5:6] == e, stand[:, 1:2] + stand[:, 3:4], 0.0)
        w_copies[i][0].wait()
        pre_gate = nn(x_ref[...], gu_ref[:, at(2 * i)])
        w_copies[i][1].wait()
        pre_up = nn(x_ref[...], gu_ref[:, at(2 * i + 1)])
        w_copies[i][2].wait()
        d_raw = nn(c_ref[...], down_ref[:, at(i)])
        sig = jax.nn.sigmoid(pre_gate)
        silu = pre_gate * sig
        hidden = silu * pre_up
        product = (hidden * d_raw).astype(BF16)
        sums = nt(jnp.ones((8, width), BF16), product)[0:1]
        for k in range(2):
            gates[k] = gates[k] + jnp.where(lying[4 + k : 5 + k] == e, sums, 0.0)
        d_hidden = prob * d_raw
        slope = pre_up * sig * (1.0 + pre_gate * (1.0 - sig))
        dgu_ref[:, at(2 * i)] = (d_hidden * slope).astype(BF16)
        dgu_ref[:, at(2 * i + 1)] = (d_hidden * silu).astype(BF16)
        hp_ref[:, at(i)] = (prob * hidden).astype(BF16)
        for m, source in enumerate(
            (dgu_ref.at[:, at(2 * i)], dgu_ref.at[:, at(2 * i + 1)], hp_ref.at[:, at(i)])
        ):
            for j, place in enumerate(places):
                copy = pltpu.make_async_copy(
                    source.at[j * rows : (j + 1) * rows, :],
                    act_all.at[step, m, place : place + rows, :],
                    act_sem.at[i, m, j],
                )
                copy.start()
                act_copies.append(copy)
    for copy in acc_copies:
        copy.wait()
    for half, (left, right) in enumerate(((hp_ref, down_ref), (dgu_ref, gu_ref))):
        value = nt(left[...], right[...])
        for j, out in enumerate(outs):
            part = value[j * rows : (j + 1) * rows]
            if has_acc:
                part = part + acc_refs[j][half * rows : (half + 1) * rows, :].astype(F32)
            out[half * rows : (half + 1) * rows, :] = part.astype(out.dtype)
    for j, out in enumerate(outs):
        pair = jnp.concatenate(
            [g[:, j * rows : (j + 1) * rows] for g in gates]
            + [jnp.zeros((ROUTE_ROWS - 2, rows), F32)],
            axis=0,
        )
        pair = jnp.concatenate([pair, jnp.zeros((ROUTE_ROWS, columns - rows), F32)], axis=1)
        if has_acc:
            pair = pair + acc_refs[j][2 * rows :, :].astype(F32)
        out[2 * rows :, :] = pair.astype(out.dtype)
    for copy in t_copies + act_copies:
        copy.wait()


def block(me, steps, pays, weights, accs, shared, places, *, rows, with_t, experts, tokens):
    shards, count = len(places), len(steps)
    packs = tuple(p[1] if isinstance(p, tuple) else None for p in pays)
    pays = [p[0] if isinstance(p, tuple) else p for p in pays]
    height, columns = pays[0].shape[-2:]
    width = weights[0][1].shape[1]
    total = shards * rows
    outs = [jax.ShapeDtypeStruct((height, columns), BF16)] * shards
    filled = [jax.ShapeDtypeStruct((experts, 3, tokens, width), BF16)]
    if with_t:
        filled += [jax.ShapeDtypeStruct((columns, tokens), BF16)] * 2
    old = list(shared[: len(filled)]) if shared else []
    args = list(pays) + [w for two in weights for w in two] + list(accs or []) + old
    first = 1 + len(args) - len(old)
    scratch = [pltpu.VMEM((total, columns), BF16)] * 2
    scratch += [pltpu.VMEM((columns, n * count * width), BF16) for n in (2, 1)]
    scratch += [pltpu.VMEM((total, n * count * width), BF16) for n in (2, 1)]
    if with_t:
        scratch += [pltpu.VMEM((columns, total), BF16)] * 2
    if accs:
        scratch += [pltpu.VMEM(a.shape, BF16) for a in accs]
    dma = pltpu.SemaphoreType.DMA
    scratch += [dma((count, 3)), dma((count, 3, shards)), dma((2, shards)), dma((shards,))]
    res = pl.pallas_call(
        functools.partial(
            block_kernel, tuple(steps), packs, rows, tuple(places), bool(accs), with_t, len(old)
        ),
        out_shape=outs + filled,
        in_specs=[pl.BlockSpec(memory_space=pltpu.SMEM)]
        + [VMEM] * len(pays)
        + [ANY] * (len(args) - len(pays)),
        out_specs=[VMEM] * shards + [ANY] * len(filled),
        scratch_shapes=scratch,
        input_output_aliases={first + n: shards + n for n in range(len(old))},
        compiler_params=pltpu.CompilerParams(vmem_limit_bytes=BLOCK_VMEM),
        cost_estimate=SMALL_COST,
        name="block",
    )(me, *args)
    new = list(res[shards:])
    return res[:shards], new + list(shared[len(new) :] if shared else [])


def grad_kernel(parts, count, me_ref, *refs):
    lefts = {}
    refs = list(refs)
    if parts != (2,):
        lefts[0] = lefts[1] = refs.pop(0)
    if 2 in parts:
        lefts[2] = refs.pop(0)
    for act, out in zip(refs[:count], refs[count:]):
        for n, m in enumerate(parts):
            at = m if act.shape[1] == 3 else n
            out[n] = nn(lefts[m][...], act[0, at]).astype(out.dtype)


def grad(me, experts, act_all, xt_all, ct_all, parts):
    columns, tokens = xt_all.shape
    width = act_all.shape[3]
    part = columns // 3
    lefts = ([xt_all] if parts != (2,) else []) + ([ct_all] if 2 in parts else [])
    place = parts[0] // len(parts)
    chosen = [
        pl.BlockSpec((1, len(parts), tokens, width), functools.partial(lambda r, i: (r, place, 0, 0), r))
        for r in experts
    ]
    return pl.pallas_call(
        functools.partial(grad_kernel, parts, len(experts)),
        grid=(3,),
        out_shape=[jax.ShapeDtypeStruct((len(parts), columns, width), BF16)] * len(experts),
        in_specs=[pl.BlockSpec(memory_space=pltpu.SMEM)]
        + [pl.BlockSpec((part, tokens), lambda i: (i, 0))] * len(lefts)
        + chosen,
        out_specs=[pl.BlockSpec((len(parts), part, width), lambda i: (0, i, 0))] * len(experts),
        compiler_params=pltpu.CompilerParams(vmem_limit_bytes=VMEM_LIMIT),
        cost_estimate=SMALL_COST,
        name="grad",
    )(me, *lefts, *[act_all] * len(experts))


def final_kernel(places, turned, count, *refs):
    parts, outs = refs[:count], refs[count:]
    for n, out in enumerate(outs):
        value = parts[0][places[0][n]].astype(F32)
        for part, at in zip(parts[1:], places[1:]):
            value = value + part[at[n]].astype(F32)
        out[0] = value.T if turned else value


def final_sum(parts, places, turned):
    _, columns, width = parts[0].shape
    part = columns // 3
    if turned:
        shape, spec = (1, width, columns), pl.BlockSpec((1, width, part), lambda i: (0, 0, i))
    else:
        shape, spec = (1, columns, width), pl.BlockSpec((1, part, width), lambda i: (0, i, 0))
    return pl.pallas_call(
        functools.partial(final_kernel, places, turned, len(parts)),
        grid=(3,),
        out_shape=[jax.ShapeDtypeStruct(shape, F32)] * len(places[0]),
        in_specs=[pl.BlockSpec((p.shape[0], part, width), lambda i: (0, i, 0)) for p in parts],
        out_specs=[spec] * len(places[0]),
        compiler_params=pltpu.CompilerParams(vmem_limit_bytes=VMEM_LIMIT),
        cost_estimate=SMALL_COST,
        name="final",
    )(*parts)


def per_device(tokens, gate_probs, expert_ids, cotangent, gate_weight, up_weight, down_weight):
    rows, columns = tokens.shape
    experts = lax.axis_size("expert")
    inner = inner_size(lax.axis_size("fsdp"))
    outer = lax.axis_size("fsdp") // inner
    me = lax.axis_index("expert").astype(jnp.int32).reshape(1)

    high = lax.reduce_precision(gate_probs, 8, 7)
    route = jnp.concatenate([high, gate_probs - high, expert_ids.astype(F32)], axis=1).T
    route = jnp.pad(route, ((0, ROUTE_ROWS - route.shape[0]), (0, columns - rows))).astype(BF16)
    own_pay = jnp.concatenate([tokens, cotangent, route], axis=0)

    beside = lambda v: [hop(v, "fsdp", j) for j in range(1, inner)]
    near, far = [0, 1], list(range(2, experts))
    size = dict(experts=experts, tokens=outer * inner * rows, rows=rows)
    own_w = [jnp.stack([gate_weight[0], up_weight[0]]), down_weight[0].T]
    weights = {r: [None] * 2 for r in range(experts)}
    weights[0] = own_w
    pays, keep, done, shared = {}, {}, {}, None
    place = lambda k, j: (k * inner + j) * rows

    def compute(steps, shards, tick, with_t):
        nonlocal shared
        accs = None if with_t else [keep[s] for s in shards]
        packed, seen = [], {}
        for s in shards:
            p = pays[s]
            if isinstance(p, tuple):
                if id(p[0]) in seen:
                    seen[id(p[0])][1].append(p[1])
                    continue
                p = (p[0], [p[1]])
                seen[id(p[0])] = p
            packed.append(p)
        packed = [(p[0], tuple(p[1])) if isinstance(p, tuple) else p for p in packed]
        if shared:
            tick = after(me, tick, shared[0])
        outs, shared = block(
            tick, steps, packed, [weights[r] for r in steps], accs, shared,
            [place(*s) for s in shards], with_t=with_t, **size,
        )
        for s, out in zip(shards, outs):
            (done if steps[-1] == far[-1] else keep)[s] = out

    row_of = lambda k: [(k, j) for j in range(inner)]

    first = hop(own_pay, "fsdp", inner)
    second = hop(own_pay, "fsdp", 2 * inner)
    for j, p in enumerate([own_pay] + beside(own_pay)):
        pays[0, j] = p
    for r in far[::2]:
        weights[r][0] = hop(own_w[0], "expert", r)
    weights[1] = [hop(w, "expert", 1) for w in own_w]
    compute(near, row_of(0), me, True)
    gus = [weights[r][0] for r in far[::2]]
    first, second, gus, shared = lax.optimization_barrier((first, second, gus, shared))

    pays[1, 0], pays[2, 0] = first, second
    pair = beside(jnp.stack([first, second]))
    for j, p in enumerate(pair):
        pays[1, j + 1], pays[2, j + 1] = (p, 0), (p, 1)
    third = hop(second, "fsdp", inner)
    for r, gu in zip(far[::2], gus):
        weights[r][0] = gu
        weights[r + 1][0] = hop(gu, "expert", 1)
        weights[r][1] = hop(after(own_w[1], gu), "expert", r)
    split = inner == 2
    if split:
        compute(near, [(1, 0), (2, 0)], me, True)
    downs = [weights[r][1] for r in far[::2]]
    gus = [weights[r + 1][0] for r in far[::2]]
    third, downs, gus, shared = lax.optimization_barrier((third, downs, gus, shared))

    for j, p in enumerate([third] + beside(third)):
        pays[3, j] = p
    for r, gu, down in zip(far[::2], gus, downs):
        weights[r][1] = down
        weights[r + 1] = [gu, hop(down, "expert", 1)]
    if split:
        compute(far, row_of(0) + [(1, 0), (2, 0)], me, False)
        compute(near, [(1, 1), (2, 1)], me, True)
        compute(far, [(1, 1), (2, 1)], me, False)
    else:
        compute(far, row_of(0), me, False)
        for k in (1, 2):
            compute(near, row_of(k), me, True)
            compute(far, row_of(k), me, False)
    compute(near + far, row_of(3), me, True)

    small = lambda v: v.astype(BF16)

    def join(k, got):
        total = done[k, 0].astype(F32)
        for g in got:
            total = total + g.astype(F32)
        return total

    def sends(k, *earlier):
        return [
            hop(after(done[k, j], *earlier) if earlier else done[k, j], "fsdp", j)
            for j in range(1, inner)
        ]

    act_all, xt_all, ct_all = shared
    back2, back3 = sends(2), sends(3)
    order = far[::-1]
    far_down = dict(zip(order, grad(after(me, act_all), order, act_all, xt_all, ct_all, (2,))))
    other_down = [hop(far_down[r + 1], "expert", 1) for r in far[::2]]
    tick = after(me, [far_down[r] for r in far])
    far_gu = dict(zip(order, grad(tick, order, act_all, xt_all, ct_all, (0, 1))))
    other_gu = [hop(far_gu[r + 1], "expert", 1) for r in far[::2]]
    other_down, back2 = lax.optimization_barrier((other_down, back2, [far_gu[r] for r in far]))[:2]
    arrived_down, arrived_gu = [], []
    for r, other in zip(far[::2], other_down):
        chip = small(far_down[r].astype(F32) + other.astype(F32))
        arrived_down.append(hop(chip, "expert", r))
    back1 = sends(1, back2, chip)
    sum3 = small(join(3, after(back3, chip)))
    up3 = hop(sum3, "fsdp", inner)
    near_grads = grad(after(me, sum3), near[::-1], act_all, xt_all, ct_all, (0, 1, 2))
    up3, back1, arrived_down, other_gu, near_grads = lax.optimization_barrier(
        (up3, back1, arrived_down, other_gu, near_grads)
    )
    sum2 = small(join(2, back2 + [up3]))
    home2 = hop(sum2, "fsdp", 2 * inner)
    sum1 = small(join(1, back1))
    home1 = hop(sum1, "fsdp", inner)
    back0 = sends(0, back1)
    for r, other in zip(far[::2], other_gu):
        chip = small(far_gu[r].astype(F32) + other.astype(F32))
        arrived_gu.append(hop(chip, "expert", r))
    other_near = hop(near_grads[0], "expert", 1)
    sum0 = join(0, back0)
    for got in (home1, home2):
        sum0 = sum0 + got.astype(F32)
    chip = small(near_grads[1].astype(F32) + other_near.astype(F32))
    (down,) = final_sum([chip] + arrived_down, [(2,)] + [(0,)] * len(arrived_down), True)
    mixed, d_tokens = small(sum0[:rows]), small(sum0[rows : 2 * rows])
    d_gates = sum0[2 * rows : 2 * rows + 2, :rows].T
    gate, up = final_sum([chip] + arrived_gu, [(0, 1)] * (1 + len(arrived_gu)), False)
    return mixed, d_tokens, d_gates, gate, up, down


def solution(mesh):
    tok = P(("expert", "fsdp"), None)
    col = P("expert", None, "fsdp")
    row = P("expert", "fsdp", None)
    return jax.shard_map(
        per_device,
        mesh=mesh,
        in_specs=(tok, tok, tok, tok, col, col, row),
        out_specs=(tok, tok, tok, col, col, row),
        check_vma=False,
    )
```

profile of v0, /device:TPU:0, one launch (start us, length us, event | category | flops | bytes accessed | tf_op | source)
XLA Modules:
  0.0 222.5 jit_solution(8430743880597660871)
XLA Ops:
  0.6 1.3 constant_dynamic-update-slice_fusion.1
  1.9 0.1 copy-done.16
  2.1 0.5 collective-permute-start.4
  2.6 2.6 %collective-permute-start.2 = (bf16[2,1536,256]{2,1,0:T(8,128)(2,1)S(1)}, bf16[2,1536,256]{2,1,0:T(8,128)(2,1)}, u32[]{:S(2)}, u32[]{:S(2)}) collective-permute-start(bf16[2,1536,256]{2,1,0:T(8,128)(2,1)S(1)} %constant_dynamic-update-slice_fusion.refs_2_.refs_1_), channel_id=1, source_target_pairs={{0,16},{8,24},{16,0},{24,8},{1,17},{9,25},{17,1},{25,9},{2,18},{10... | collective-permute-start | bytes 4718600 | tf_op jit(solution)/shard_map/ppermute | solution.py:21
  5.2 2.3 %copy.24 = bf16[1,256,1536]{1,2,0:T(8,128)(2,1)} copy(bf16[1,256,1536]{2,1,0:T(8,128)(2,1)} %param.13) | data formatting | bytes 1572864 | tf_op args[6]
  7.5 0.2 collective-permute-start.5
  7.7 2.0 fusion.1.refs_0_
  9.6 1.5 collective-permute-start.3
  11.2 1.6 collective-permute-start
  12.7 2.6 %collective-permute-start.1 = (bf16[264,1536]{1,0:T(8,128)(2,1)}, bf16[264,1536]{1,0:T(8,128)(2,1)}, u32[]{:S(2)}, u32[]{:S(2)}) collective-permute-start(bf16[264,1536]{1,0:T(8,128)(2,1)} %fusion.1.refs_0_), channel_id=1, source_target_pairs={{0,4},{1,5},{2,6},{3,7},{4,0},{5,1},{6,2},{7,3},{8,12},{9,13},{10,... | collective-permute-start | bytes 2433032 | tf_op jit(solution)/shard_map/ppermute | solution.py:21
  15.3 14.9 %collective-permute-done.3.refs_1_ = bf16[264,1536]{1,0:T(8,128)(2,1)} collective-permute-done((bf16[264,1536]{1,0:T(8,128)(2,1)}, bf16[264,1536]{1,0:T(8,128)(2,1)}, u32[]{:S(2)}, u32[]{:S(2)}) %collective-permute-start.3) | collective-permute-done | bytes 811040 | tf_op jit(solution)/shard_map/ppermute | solution.py:21
  30.3 1.1 copy-done.4
  31.4 8.9 %block.6 = (bf16[264,1536]{1,0:T(8,128)(2,1)}, bf16[264,1536]{1,0:T(8,128)(2,1)}, bf16[4,3,1024,256]{3,2,1,0:T(8,128)(2,1)}, bf16[1536,1024]{1,0:T(8,128)(2,1)}, bf16[1536,1024]{1,0:T(8,128)(2,1)}) custom-call(s32[1]{0:T(128)} %bitcast.me_ref, bf16[264,1536]{1,0:T(8,128)(2,1)} %fusion.1.refs_0_, bf16[264,1536]{1,0:T(8,128)(2,1)} %collective-permute-done.3.refs_1_, ...), custom_call_target="tpu_custom_call" | custom-call | flops 1000 | bytes 1000 | tf_op jit(solution)/shard_map/block/pallas_call | solution.py:182
  40.3 8.5 %collective-permute-done.refs_0_.refs_2_ = bf16[264,1536]{1,0:T(8,128)(2,1)} collective-permute-done((bf16[264,1536]{1,0:T(8,128)(2,1)}, bf16[264,1536]{1,0:T(8,128)(2,1)}, u32[]{:S(2)}, u32[]{:S(2)}) %collective-permute-start) | collective-permute-done | bytes 811040 | tf_op jit(solution)/shard_map/ppermute | solution.py:21
  48.8 2.4 %collective-permute-done.1.refs_1_.refs_3_ = bf16[264,1536]{1,0:T(8,128)(2,1)} collective-permute-done((bf16[264,1536]{1,0:T(8,128)(2,1)}, bf16[264,1536]{1,0:T(8,128)(2,1)}, u32[]{:S(2)}, u32[]{:S(2)}) %collective-permute-start.1) | collective-permute-done | bytes 811040 | tf_op jit(solution)/shard_map/ppermute | solution.py:21
  51.2 1.6 pad_maximum_fusion
  52.8 0.6 collective-permute-start.10
  53.3 0.4 collective-permute-start.6
  53.8 0.5 collective-permute-start.7
  54.3 8.8 %block.7 = (bf16[264,1536]{1,0:T(8,128)(2,1)}, bf16[264,1536]{1,0:T(8,128)(2,1)}, bf16[4,3,1024,256]{3,2,1,0:T(8,128)(2,1)}, bf16[1536,1024]{1,0:T(8,128)(2,1)}, bf16[1536,1024]{1,0:T(8,128)(2,1)}) custom-call(s32[1]{0:T(128)} %bitcast.me_ref, ...), custom_call_target="tpu_custom_call", output_to_operand_aliasing={{2}: (7, {}), {3}: (8, {}), {4}: (9, {})} | custom-call | flops 1000 | bytes 1000 | tf_op jit(solution)/shard_map/block/pallas_call | solution.py:182
  63.1 10.0 %collective-permute-done.7.refs_5_.refs_2_.refs_7_ = bf16[1536,256]{1,0:T(8,128)(2,1)S(1)} collective-permute-done((bf16[1536,256]{1,0:T(8,128)(2,1)S(1)}, bf16[1536,256]{1,0:T(8,128)(2,1)S(1)}, u32[]{:S(2)}, u32[]{:S(2)}) %collective-permute-start.7) | collective-permute-done | bytes 786464 | tf_op jit(solution)/shard_map/ppermute | solution.py:21
  73.2 0.6 collective-permute-done.6.refs_0_
  73.8 1.6 collective-permute-start.11
  75.4 0.7 collective-permute-done.9.refs_7_.refs_4_.refs_9_
  76.1 0.9 copy-done.8
  77.0 14.6 %block.8 = (bf16[264,1536]{1,0:T(8,128)(2,1)}, bf16[264,1536]{1,0:T(8,128)(2,1)}, bf16[264,1536]{1,0:T(8,128)(2,1)}, bf16[264,1536]{1,0:T(8,128)(2,1)}, bf16[4,3,1024,256]{3,2,1,0:T(8,128)(2,1)}) custom-call(s32[1]{0:T(128)} %bitcast.me_ref, bf16[264,1536]{1,0:T(8,128)(2,1)} %fusion.1.refs_0_, ...), custom_call_target="tpu_custom_call", output_to_operand_aliasing={{4}: (13, {})} | custom-call | flops 1000 | bytes 1000 | tf_op jit(solution)/shard_map/block/pallas_call | solution.py:182
  91.7 1.3 copy-done.9
  92.9 8.9 %block.9 = (bf16[264,1536]{1,0:T(8,128)(2,1)}, bf16[264,1536]{1,0:T(8,128)(2,1)}, bf16[4,3,1024,256]{3,2,1,0:T(8,128)(2,1)}, bf16[1536,1024]{1,0:T(8,128)(2,1)}, bf16[1536,1024]{1,0:T(8,128)(2,1)}) custom-call(s32[1]{0:T(128)} %bitcast.me_ref, bf16[2,264,1536]{2,1,0:T(8,128)(2,1)} %copy-done.9, ...), custom_call_target="tpu_custom_call", output_to_operand_aliasing={{2}: (6, {}), {3}: (7, {}), {4}: (8, {})} | custom-call | flops 1000 | bytes 1000 | tf_op jit(solution)/shard_map/block/pallas_call | solution.py:182
  101.8 9.0 %block.10 = (bf16[264,1536]{1,0:T(8,128)(2,1)}, bf16[264,1536]{1,0:T(8,128)(2,1)}, bf16[4,3,1024,256]{3,2,1,0:T(8,128)(2,1)}) custom-call(s32[1]{0:T(128)} %bitcast.me_ref, bf16[2,264,1536]{2,1,0:T(8,128)(2,1)} %copy-done.9, bf16[2,1536,256]{2,1,0:T(8,128)(2,1)} %collective-permute-done.2.refs_4_.refs_1_.refs_6_, ...), custom_call_target="tpu_custom_call", output_to_operand_aliasing={{2}: (8, {})} | custom-call | flops 1000 | bytes 1000 | tf_op jit(solution)/shard_map/block/pallas_call | solution.py:182
  110.9 1.6 collective-permute-start.14
  112.5 1.0 copy-done.11
  113.5 14.2 %block.11 = (bf16[264,1536]{1,0:T(8,128)(2,1)}, bf16[264,1536]{1,0:T(8,128)(2,1)}, bf16[4,3,1024,256]{3,2,1,0:T(8,128)(2,1)}, bf16[1536,1024]{1,0:T(8,128)(2,1)}, bf16[1536,1024]{1,0:T(8,128)(2,1)}) custom-call(s32[1]{0:T(128)} %bitcast.me_ref, bf16[264,1536]{1,0:T(8,128)(2,1)} %copy-done.10, ...), custom_call_target="tpu_custom_call", output_to_operand_aliasing={{2}: (11, {}), {3}: (12, {}), {4}: (13, {})} | custom-call | flops 1000 | bytes 1000 | tf_op jit(solution)/shard_map/block/pallas_call | solution.py:182
  127.6 2.8 %copy-done = bf16[4,3,1024,256]{3,2,1,0:T(8,128)(2,1)S(1)} copy-done((bf16[4,3,1024,256]{3,2,1,0:T(8,128)(2,1)S(1)}, bf16[4,3,1024,256]{3,2,1,0:T(8,128)(2,1)}, u32[]{:S(2)}) %copy-start) | copy-done | bytes 6291480
  130.4 1.9 copy-done.2
  132.3 2.1 grad.3
  134.5 0.1 collective-permute-start.13
  134.6 0.6 collective-permute-start.12
  135.1 3.9 %grad.4 = (bf16[2,1536,256]{2,1,0:T(8,128)(2,1)S(1)}, bf16[2,1536,256]{2,1,0:T(8,128)(2,1)S(1)}) custom-call(s32[1]{0:T(128)} %bitcast.me_ref, bf16[1536,1024]{1,0:T(8,128)(2,1)S(1)} %copy-done.1, bf16[4,3,1024,256]{3,2,1,0:T(8,128)(2,1)S(1)} %copy-done, bf16[4,3,1024,256]{3,2,1,0:T(8,128)(2,1)S(1)} %copy-done), custom_call_target="tpu_custom_call" | custom-call | flops 1000 | bytes 1000 | tf_op jit(solution)/shard_map/grad/pallas_call | solution.py:224
  139.1 0.2 collective-permute-start.18
  139.3 0.2 add_convert_fusion.5
  139.5 0.7 copy-done.20
  140.2 1.5 collective-permute-start.16
  141.7 13.8 %collective-permute-done.12 = bf16[264,1536]{1,0:T(8,128)(2,1)S(1)} collective-permute-done((bf16[264,1536]{1,0:T(8,128)(2,1)S(1)}, bf16[264,1536]{1,0:T(8,128)(2,1)S(1)}, u32[]{:S(2)}, u32[]{:S(2)}) %collective-permute-start.12) | collective-permute-done | bytes 811040 | tf_op jit(solution)/shard_map/ppermute | solution.py:21
  155.5 0.2 add_convert_fusion.4
  155.8 1.1 collective-permute-start.15
  156.9 0.5 collective-permute-start.17
  157.4 5.7 %grad.5 = (bf16[3,1536,256]{2,1,0:T(8,128)(2,1)S(1)}, bf16[3,1536,256]{2,1,0:T(8,128)(2,1)S(1)}) custom-call(s32[1]{0:T(128)} %bitcast.me_ref, bf16[1536,1024]{1,0:T(8,128)(2,1)S(1)} %copy-done.1, bf16[1536,1024]{1,0:T(8,128)(2,1)S(1)} %copy-done.2, bf16[4,3,1024,256]{3,2,1,0:T(8,128)(2,1)S(1)} %copy-done, bf16[4,3,1024,256]{3,2,1,0:T(8,128)(2,1)S(1)} %copy-done), custom_call_target="tpu_custom_call" | custom-call | flops 1000 | bytes 1000 | tf_op jit(solution)/shard_map/grad/pallas_call | solution.py:224
  163.1 12.1 %collective-permute-done.17.refs_1_ = bf16[1,1536,256]{2,1,0:T(8,128)(2,1)S(1)} collective-permute-done((bf16[1,1536,256]{2,1,0:T(8,128)(2,1)S(1)}, bf16[1,1536,256]{2,1,0:T(8,128)(2,1)S(1)}, u32[]{:S(2)}, u32[]{:S(2)}) %collective-permute-start.17) | collective-permute-done | bytes 786464 | tf_op jit(solution)/shard_map/ppermute | solution.py:21
  175.2 0.6 collective-permute-start.19
  175.8 0.2 add_convert_fusion.3
  176.0 1.1 collective-permute-start.20
  177.1 0.3 add_convert_fusion.2
  177.4 2.1 collective-permute-start.21
  179.5 0.4 add_convert_fusion.1
  179.9 0.6 collective-permute-start.23
  180.5 15.3 %collective-permute-done.19 = bf16[264,1536]{1,0:T(8,128)(2,1)S(1)} collective-permute-done((bf16[264,1536]{1,0:T(8,128)(2,1)S(1)}, bf16[264,1536]{1,0:T(8,128)(2,1)S(1)}, u32[]{:S(2)}, u32[]{:S(2)}) %collective-permute-start.19) | collective-permute-done | bytes 811040 | tf_op jit(solution)/shard_map/ppermute | solution.py:21
  195.7 17.4 %collective-permute-done.20 = bf16[264,1536]{1,0:T(8,128)(2,1)S(1)} collective-permute-done((bf16[264,1536]{1,0:T(8,128)(2,1)S(1)}, bf16[264,1536]{1,0:T(8,128)(2,1)S(1)}, u32[]{:S(2)}, u32[]{:S(2)}) %collective-permute-start.20) | collective-permute-done | bytes 811040 | tf_op jit(solution)/shard_map/ppermute | solution.py:21
  213.1 2.5 %collective-permute-done.21 = bf16[264,1536]{1,0:T(8,128)(2,1)S(1)} collective-permute-done((bf16[264,1536]{1,0:T(8,128)(2,1)S(1)}, bf16[264,1536]{1,0:T(8,128)(2,1)S(1)}, u32[]{:S(2)}, u32[]{:S(2)}) %collective-permute-start.21) | collective-permute-done | bytes 811040 | tf_op jit(solution)/shard_map/ppermute | solution.py:21
  215.6 0.4 fusion.3
  216.0 0.6 slice_bitcast_fusion
  216.6 0.9 fusion.4
  217.5 0.5 add_convert_fusion.refs_0_
  218.1 2.1 final.3
  220.2 2.2 %final.2 = (f32[1,1536,256]{2,1,0:T(8,128)}, f32[1,1536,256]{2,1,0:T(8,128)}) custom-call(bf16[3,1536,256]{2,1,0:T(8,128)(2,1)S(1)} %add_convert_fusion.refs_0_, bf16[2,1536,256]{2,1,0:T(8,128)(2,1)S(1)} %collective-permute-done.23.refs_1_), custom_call_target="tpu_custom_call" | custom-call | flops 1000 | bytes 1000 | tf_op jit(solution)/shard_map/final/pallas_call | solution.py:254
  (58 shorter events, 0.3 us)
Async XLA Ops:
  0.6 1.4 copy-start.16
  2.0 5.6 %copy-start.22 = (s32[128,2]{0,1:T(2,128)S(1)}, s32[128,2]{0,1:T(2,128)}, u32[]{:S(2)}) copy-start(s32[128,2]{0,1:T(2,128)} %param.9) | copy-start | bytes 3076
  2.0 5.6 %copy-start.18 = (f32[128,2]{0,1:T(2,128)S(1)}, f32[128,2]{0,1:T(2,128)}, u32[]{:S(2)}) copy-start(f32[128,2]{0,1:T(2,128)} %param.8) | copy-start | bytes 3076
  2.0 5.7 %copy-start.17 = (bf16[128,1536]{1,0:T(8,128)(2,1)S(1)}, bf16[128,1536]{1,0:T(8,128)(2,1)}, u32[]{:S(2)}) copy-start(bf16[128,1536]{1,0:T(8,128)(2,1)} %param.10) | copy-start | bytes 1179652
  2.1 28.2 %copy-start.3 = (bf16[2,1536,256]{2,1,0:T(8,128)(2,1)}, bf16[2,1536,256]{2,1,0:T(8,128)(2,1)S(1)}, u32[]{:S(2)}) copy-start(bf16[2,1536,256]{2,1,0:T(8,128)(2,1)S(1)} %constant_dynamic-update-slice_fusion.refs_2_.refs_1_) | copy-start | bytes 4718596
  2.1 28.2 %collective-permute-start.4 = (bf16[2,1536,256]{2,1,0:T(8,128)(2,1)S(1)}, bf16[2,1536,256]{2,1,0:T(8,128)(2,1)S(1)}, u32[]{:S(2)}, u32[]{:S(2)}) collective-permute-start(bf16[2,1536,256]{2,1,0:T(8,128)(2,1)S(1)} %constant_dynamic-update-slice_fusion.refs_2_.refs_1_), channel_id=1, source_target_pairs={{0,8},{8,0},{16,24},{24,16},{1,9},{9,1},{17,25},{25,17},{2,10},{10... | collective-permute-start | bytes 4718600 | tf_op jit(solution)/shard_map/ppermute | solution.py:21
  2.6 48.6 %collective-permute-start.2 = (bf16[2,1536,256]{2,1,0:T(8,128)(2,1)S(1)}, bf16[2,1536,256]{2,1,0:T(8,128)(2,1)}, u32[]{:S(2)}, u32[]{:S(2)}) collective-permute-start(bf16[2,1536,256]{2,1,0:T(8,128)(2,1)S(1)} %constant_dynamic-update-slice_fusion.refs_2_.refs_1_), channel_id=1, source_target_pairs={{0,16},{8,24},{16,0},{24,8},{1,17},{9,25},{17,1},{25,9},{2,18},{10... | collective-permute-start | bytes 4718600 | tf_op jit(solution)/shard_map/ppermute | solution.py:21
  7.5 5.3 %collective-permute-start.5 = (bf16[1536,256]{1,0:T(8,128)(2,1)}, bf16[1536,256]{1,0:T(8,128)(2,1)}, u32[]{:S(2)}, u32[]{:S(2)}) collective-permute-start(bf16[1536,256]{1,0:T(8,128)(2,1)} %bitcast.10), channel_id=1, source_target_pairs={{0,8},{8,0},{16,24},{24,16},{1,9},{9,1},{17,25},{25,17},{2,10},{10... | collective-permute-start | bytes 2359304 | tf_op jit(solution)/shard_map/ppermute | solution.py:21
  9.6 20.6 %collective-permute-start.3 = (bf16[264,1536]{1,0:T(8,128)(2,1)}, bf16[264,1536]{1,0:T(8,128)(2,1)}, u32[]{:S(2)}, u32[]{:S(2)}) collective-permute-start(bf16[264,1536]{1,0:T(8,128)(2,1)} %fusion.1.refs_0_), channel_id=1, source_target_pairs={{0,1},{1,0},{2,3},{3,2},{4,5},{5,4},{6,7},{7,6},{8,9},{9,8},{10,11... | collective-permute-start | bytes 2433032 | tf_op jit(solution)/shard_map/ppermute | solution.py:21
  11.2 37.6 %collective-permute-start = (bf16[264,1536]{1,0:T(8,128)(2,1)}, bf16[264,1536]{1,0:T(8,128)(2,1)}, u32[]{:S(2)}, u32[]{:S(2)}) collective-permute-start(bf16[264,1536]{1,0:T(8,128)(2,1)} %fusion.1.refs_0_), channel_id=1, source_target_pairs={{0,2},{1,3},{2,0},{3,1},{4,6},{5,7},{6,4},{7,5},{8,10},{9,11},{10,... | collective-permute-start | bytes 2433032 | tf_op jit(solution)/shard_map/ppermute | solution.py:21
  12.7 38.4 %collective-permute-start.1 = (bf16[264,1536]{1,0:T(8,128)(2,1)}, bf16[264,1536]{1,0:T(8,128)(2,1)}, u32[]{:S(2)}, u32[]{:S(2)}) collective-permute-start(bf16[264,1536]{1,0:T(8,128)(2,1)} %fusion.1.refs_0_), channel_id=1, source_target_pairs={{0,4},{1,5},{2,6},{3,7},{4,0},{5,1},{6,2},{7,3},{8,12},{9,13},{10,... | collective-permute-start | bytes 2433032 | tf_op jit(solution)/shard_map/ppermute | solution.py:21
  30.3 1.1 copy-start.4
  51.1 22.6 %collective-permute-start.8 = (bf16[2,1536,256]{2,1,0:T(8,128)(2,1)}, bf16[2,1536,256]{2,1,0:T(8,128)(2,1)S(1)}, u32[]{:S(2)}, u32[]{:S(2)}) collective-permute-start(bf16[2,1536,256]{2,1,0:T(8,128)(2,1)} %collective-permute-done.2.refs_4_.refs_1_.refs_6_), channel_id=1, source_target_pairs={{0,8},{8,0},{16,24},{24,16},{1,9},{9,1},{17,25},{25,17},{2,10},{10... | collective-permute-start | bytes 4718600 | tf_op jit(solution)/shard_map/ppermute | solution.py:21
  51.1 2.6 %copy-start.5 = (bf16[1,256,1536]{1,2,0:T(8,128)(2,1)S(1)}, bf16[1,256,1536]{1,2,0:T(8,128)(2,1)}, u32[]{:S(2)}) copy-start(bf16[1,256,1536]{1,2,0:T(8,128)(2,1)} %copy.24) | copy-start | bytes 2359300
  52.8 38.9 %collective-permute-start.10 = (bf16[2,264,1536]{2,1,0:T(8,128)(2,1)S(1)}, bf16[2,264,1536]{2,1,0:T(8,128)(2,1)S(1)}, u32[]{:S(2)}, u32[]{:S(2)}) collective-permute-start(bf16[2,264,1536]{2,1,0:T(8,128)(2,1)S(1)} %pad_maximum_fusion), channel_id=1, source_target_pairs={{0,1},{1,0},{2,3},{3,2},{4,5},{5,4},{6,7},{7,6},{8,9},{9,8},{10,11... | collective-permute-start | bytes 4866056 | tf_op jit(solution)/shard_map/ppermute | solution.py:21
  53.3 20.4 %collective-permute-start.6 = (bf16[264,1536]{1,0:T(8,128)(2,1)}, bf16[264,1536]{1,0:T(8,128)(2,1)S(1)}, u32[]{:S(2)}, u32[]{:S(2)}) collective-permute-start(bf16[264,1536]{1,0:T(8,128)(2,1)} %collective-permute-done.1.refs_1_.refs_3_), channel_id=1, source_target_pairs={{0,2},{1,3},{2,0},{3,1},{4,6},{5,7},{6,4},{7,5},{8,10},{9,11},{10,... | collective-permute-start | bytes 2433032 | tf_op jit(solution)/shard_map/ppermute | solution.py:21
  53.8 19.4 %collective-permute-start.7 = (bf16[1536,256]{1,0:T(8,128)(2,1)S(1)}, bf16[1536,256]{1,0:T(8,128)(2,1)S(1)}, u32[]{:S(2)}, u32[]{:S(2)}) collective-permute-start(bf16[1536,256]{1,0:T(8,128)(2,1)S(1)} %bitcast.15), channel_id=1, source_target_pairs={{0,16},{8,24},{16,0},{24,8},{1,17},{9,25},{17,1},{25,9},{2,18},{10... | collective-permute-start | bytes 2359304 | tf_op jit(solution)/shard_map/ppermute | solution.py:21
  73.2 2.9 %copy-start.7 = (bf16[1536,256]{1,0:T(8,128)(2,1)}, bf16[1536,256]{1,0:T(8,128)(2,1)S(1)}, u32[]{:S(2)}) copy-start(bf16[1536,256]{1,0:T(8,128)(2,1)S(1)} %collective-permute-done.7.refs_5_.refs_2_.refs_7_) | copy-start | bytes 2359300
  73.7 17.9 %copy-start.10 = (bf16[264,1536]{1,0:T(8,128)(2,1)}, bf16[264,1536]{1,0:T(8,128)(2,1)S(1)}, u32[]{:S(2)}) copy-start(bf16[264,1536]{1,0:T(8,128)(2,1)S(1)} %collective-permute-done.6.refs_0_) | copy-start | bytes 2433028
  73.8 2.4 %copy-start.6 = (bf16[2,1536,256]{2,1,0:T(8,128)(2,1)}, bf16[2,1536,256]{2,1,0:T(8,128)(2,1)S(1)}, u32[]{:S(2)}) copy-start(bf16[2,1536,256]{2,1,0:T(8,128)(2,1)S(1)} %collective-permute-done.8.refs_6_.refs_3_.refs_8_) | copy-start | bytes 4718596
  73.8 2.3 %collective-permute-start.9 = (bf16[1536,256]{1,0:T(8,128)(2,1)S(1)}, bf16[1536,256]{1,0:T(8,128)(2,1)S(1)}, u32[]{:S(2)}, u32[]{:S(2)}) collective-permute-start(bf16[1536,256]{1,0:T(8,128)(2,1)S(1)} %collective-permute-done.7.refs_5_.refs_2_.refs_7_), channel_id=1, source_target_pairs={{0,8},{8,0},{16,24},{24,16},{1,9},{9,1},{17,25},{25,17},{2,10},{10... | collective-permute-start | bytes 2359304 | tf_op jit(solution)/shard_map/ppermute | solution.py:21
  73.8 38.6 %collective-permute-start.11 = (bf16[264,1536]{1,0:T(8,128)(2,1)S(1)}, bf16[264,1536]{1,0:T(8,128)(2,1)S(1)}, u32[]{:S(2)}, u32[]{:S(2)}) collective-permute-start(bf16[264,1536]{1,0:T(8,128)(2,1)S(1)} %collective-permute-done.6.refs_0_), channel_id=1, source_target_pairs={{0,1},{1,0},{2,3},{3,2},{4,5},{5,4},{6,7},{7,6},{8,9},{9,8},{10,11... | collective-permute-start | bytes 2433032 | tf_op jit(solution)/shard_map/ppermute | solution.py:21
  76.1 0.9 copy-start.8
  91.7 1.3 copy-start.9
  110.9 28.4 %collective-permute-start.14 = (bf16[264,1536]{1,0:T(8,128)(2,1)}, bf16[264,1536]{1,0:T(8,128)(2,1)S(1)}, u32[]{:S(2)}, u32[]{:S(2)}) collective-permute-start(bf16[264,1536]{1,0:T(8,128)(2,1)} %get-tuple-element.118), channel_id=1, source_target_pairs={{0,1},{1,0},{2,3},{3,2},{4,5},{5,4},{6,7},{7,6},{8,9},{9,8},{10,11... | collective-permute-start | bytes 2433032 | tf_op jit(solution)/shard_map/ppermute | solution.py:21
  112.5 1.0 copy-start.11
  127.6 2.8 %copy-start = (bf16[4,3,1024,256]{3,2,1,0:T(8,128)(2,1)S(1)}, bf16[4,3,1024,256]{3,2,1,0:T(8,128)(2,1)}, u32[]{:S(2)}) copy-start(bf16[4,3,1024,256]{3,2,1,0:T(8,128)(2,1)} %get-tuple-element.113.refs_1_.refs_2_.refs_3_) | copy-start | bytes 18874372
  130.4 1.9 copy-start.2
  132.3 2.2 %copy-start.21 = (bf16[264,1536]{1,0:T(8,128)(2,1)S(1)}, bf16[264,1536]{1,0:T(8,128)(2,1)}, u32[]{:S(2)}) copy-start(bf16[264,1536]{1,0:T(8,128)(2,1)} %get-tuple-element.112) | copy-start | bytes 2433028
  132.3 2.8 %copy-start.1 = (bf16[1536,1024]{1,0:T(8,128)(2,1)S(1)}, bf16[1536,1024]{1,0:T(8,128)(2,1)}, u32[]{:S(2)}) copy-start(bf16[1536,1024]{1,0:T(8,128)(2,1)} %get-tuple-element.120.refs_0_) | copy-start | bytes 9437188
  134.5 4.9 %collective-permute-start.13 = (bf16[1,1536,256]{2,1,0:T(8,128)(2,1)S(1)}, bf16[1,1536,256]{2,1,0:T(8,128)(2,1)S(1)}, u32[]{:S(2)}, u32[]{:S(2)}) collective-permute-start(bf16[1,1536,256]{2,1,0:T(8,128)(2,1)S(1)} %get-tuple-element.117), channel_id=1, source_target_pairs={{0,8},{8,0},{16,24},{24,16},{1,9},{9,1},{17,25},{25,17},{2,10},{10... | collective-permute-start | bytes 2359304 | tf_op jit(solution)/shard_map/ppermute | solution.py:21
  134.6 20.9 %collective-permute-start.12 = (bf16[264,1536]{1,0:T(8,128)(2,1)S(1)}, bf16[264,1536]{1,0:T(8,128)(2,1)S(1)}, u32[]{:S(2)}, u32[]{:S(2)}) collective-permute-start(bf16[264,1536]{1,0:T(8,128)(2,1)S(1)} %copy-done.21), channel_id=1, source_target_pairs={{0,1},{1,0},{2,3},{3,2},{4,5},{5,4},{6,7},{7,6},{8,9},{9,8},{10,11... | collective-permute-start | bytes 2433032 | tf_op jit(solution)/shard_map/ppermute | solution.py:21
  139.1 1.1 copy-start.20
  139.1 16.4 %copy-start.14 = (bf16[264,1536]{1,0:T(8,128)(2,1)S(1)}, bf16[264,1536]{1,0:T(8,128)(2,1)}, u32[]{:S(2)}) copy-start(bf16[264,1536]{1,0:T(8,128)(2,1)} %get-tuple-element.111) | copy-start | bytes 2433028
  139.1 24.0 %collective-permute-start.18 = (bf16[2,1536,256]{2,1,0:T(8,128)(2,1)S(1)}, bf16[2,1536,256]{2,1,0:T(8,128)(2,1)S(1)}, u32[]{:S(2)}, u32[]{:S(2)}) collective-permute-start(bf16[2,1536,256]{2,1,0:T(8,128)(2,1)S(1)} %get-tuple-element.122), channel_id=1, source_target_pairs={{0,8},{8,0},{16,24},{24,16},{1,9},{9,1},{17,25},{25,17},{2,10},{10... | collective-permute-start | bytes 4718600 | tf_op jit(solution)/shard_map/ppermute | solution.py:21
  140.2 35.0 %collective-permute-start.16 = (bf16[264,1536]{1,0:T(8,128)(2,1)S(1)}, bf16[264,1536]{1,0:T(8,128)(2,1)S(1)}, u32[]{:S(2)}, u32[]{:S(2)}) collective-permute-start(bf16[264,1536]{1,0:T(8,128)(2,1)S(1)} %copy-done.20), channel_id=1, source_target_pairs={{0,1},{1,0},{2,3},{3,2},{4,5},{5,4},{6,7},{7,6},{8,9},{9,8},{10,11... | collective-permute-start | bytes 2433032 | tf_op jit(solution)/shard_map/ppermute | solution.py:21
  155.7 19.5 %copy-start.19 = (bf16[264,1536]{1,0:T(8,128)(2,1)S(1)}, bf16[264,1536]{1,0:T(8,128)(2,1)}, u32[]{:S(2)}) copy-start(bf16[264,1536]{1,0:T(8,128)(2,1)} %get-tuple-element.132) | copy-start | bytes 2433028
  155.7 20.1 %copy-start.13 = (bf16[264,1536]{1,0:T(8,128)(2,1)S(1)}, bf16[264,1536]{1,0:T(8,128)(2,1)}, u32[]{:S(2)}) copy-start(bf16[264,1536]{1,0:T(8,128)(2,1)} %get-tuple-element.133) | copy-start | bytes 2433028
  155.8 19.5 %collective-permute-start.15 = (bf16[264,1536]{1,0:T(8,128)(2,1)S(1)}, bf16[264,1536]{1,0:T(8,128)(2,1)S(1)}, u32[]{:S(2)}, u32[]{:S(2)}) collective-permute-start(bf16[264,1536]{1,0:T(8,128)(2,1)S(1)} %add_convert_fusion.4), channel_id=1, source_target_pairs={{0,2},{1,3},{2,0},{3,1},{4,6},{5,7},{6,4},{7,5},{8,10},{9,11},{10,... | collective-permute-start | bytes 2433032 | tf_op jit(solution)/shard_map/ppermute | solution.py:21
  156.9 18.4 %collective-permute-start.17 = (bf16[1,1536,256]{2,1,0:T(8,128)(2,1)S(1)}, bf16[1,1536,256]{2,1,0:T(8,128)(2,1)S(1)}, u32[]{:S(2)}, u32[]{:S(2)}) collective-permute-start(bf16[1,1536,256]{2,1,0:T(8,128)(2,1)S(1)} %add_convert_fusion.5), channel_id=1, source_target_pairs={{0,16},{8,24},{16,0},{24,8},{1,17},{9,25},{17,1},{25,9},{2,18},{10... | collective-permute-start | bytes 2359304 | tf_op jit(solution)/shard_map/ppermute | solution.py:21
  163.1 14.0 %copy-start.12 = (bf16[264,1536]{1,0:T(8,128)(2,1)S(1)}, bf16[264,1536]{1,0:T(8,128)(2,1)}, u32[]{:S(2)}) copy-start(bf16[264,1536]{1,0:T(8,128)(2,1)} %get-tuple-element.134) | copy-start | bytes 2433028
  175.2 42.3 %collective-permute-start.22 = (bf16[3,1536,256]{2,1,0:T(8,128)(2,1)S(1)}, bf16[3,1536,256]{2,1,0:T(8,128)(2,1)S(1)}, u32[]{:S(2)}, u32[]{:S(2)}) collective-permute-start(bf16[3,1536,256]{2,1,0:T(8,128)(2,1)S(1)} %get-tuple-element.137), channel_id=1, source_target_pairs={{0,8},{8,0},{16,24},{24,16},{1,9},{9,1},{17,25},{25,17},{2,10},{10... | collective-permute-start | bytes 7077896 | tf_op jit(solution)/shard_map/ppermute | solution.py:21
  175.2 20.5 %collective-permute-start.19 = (bf16[264,1536]{1,0:T(8,128)(2,1)S(1)}, bf16[264,1536]{1,0:T(8,128)(2,1)S(1)}, u32[]{:S(2)}, u32[]{:S(2)}) collective-permute-start(bf16[264,1536]{1,0:T(8,128)(2,1)S(1)} %copy-done.19), channel_id=1, source_target_pairs={{0,1},{1,0},{2,3},{3,2},{4,5},{5,4},{6,7},{7,6},{8,9},{9,8},{10,11... | collective-permute-start | bytes 2433032 | tf_op jit(solution)/shard_map/ppermute | solution.py:21
  176.0 37.1 %collective-permute-start.20 = (bf16[264,1536]{1,0:T(8,128)(2,1)S(1)}, bf16[264,1536]{1,0:T(8,128)(2,1)S(1)}, u32[]{:S(2)}, u32[]{:S(2)}) collective-permute-start(bf16[264,1536]{1,0:T(8,128)(2,1)S(1)} %add_convert_fusion.3), channel_id=1, source_target_pairs={{0,2},{1,3},{2,0},{3,1},{4,6},{5,7},{6,4},{7,5},{8,10},{9,11},{10,... | collective-permute-start | bytes 2433032 | tf_op jit(solution)/shard_map/ppermute | solution.py:21
  177.4 38.3 %copy-start.15 = (bf16[264,1536]{1,0:T(8,128)(2,1)S(1)}, bf16[264,1536]{1,0:T(8,128)(2,1)}, u32[]{:S(2)}) copy-start(bf16[264,1536]{1,0:T(8,128)(2,1)} %get-tuple-element.96) | copy-start | bytes 2433028
  177.4 38.2 %collective-permute-start.21 = (bf16[264,1536]{1,0:T(8,128)(2,1)S(1)}, bf16[264,1536]{1,0:T(8,128)(2,1)S(1)}, u32[]{:S(2)}, u32[]{:S(2)}) collective-permute-start(bf16[264,1536]{1,0:T(8,128)(2,1)S(1)} %add_convert_fusion.2), channel_id=1, source_target_pairs={{0,4},{1,5},{2,6},{3,7},{4,0},{5,1},{6,2},{7,3},{8,12},{9,13},{10,... | collective-permute-start | bytes 2433032 | tf_op jit(solution)/shard_map/ppermute | solution.py:21
  179.9 40.4 %collective-permute-start.23 = (bf16[2,1536,256]{2,1,0:T(8,128)(2,1)S(1)}, bf16[2,1536,256]{2,1,0:T(8,128)(2,1)S(1)}, u32[]{:S(2)}, u32[]{:S(2)}) collective-permute-start(bf16[2,1536,256]{2,1,0:T(8,128)(2,1)S(1)} %add_convert_fusion.1), channel_id=1, source_target_pairs={{0,16},{8,24},{16,0},{24,8},{1,17},{9,25},{17,1},{25,9},{2,18},{10... | collective-permute-start | bytes 4718600 | tf_op jit(solution)/shard_map/ppermute | solution.py:21
where the time goes:
time: 223 us; the launch traced here: 222 us
  waiting for transfers between devices  98.2 us (44%)
  Pallas kernels  80.5 us (36%)
  starting transfers between devices  22.1 us (10%)
  local copies, waits for them, and re-layouts  14.9 us (7%)
  other arithmetic  5.82 us (3%)
    ppermute x24, waiting for transfers between devices, hop(): lax.ppermute(value, axis, [(i, i ^ step) for i in range(lax.axis_size(axi...  98.2 us
    pallas_call x6, Pallas kernels, block(): pl.pallas_call(functools.partial(block_kernel, tuple(steps), packs, rows,...  64.4 us
    ppermute x24, starting transfers between devices, hop(): lax.ppermute(value, axis, [(i, i ^ step) for i in range(lax.axis_size(axi...  22.1 us
    unnamed x48, local copies, waits for them, and re-layouts  13.4 us
    pallas_call x3, Pallas kernels, grad(): pl.pallas_call(functools.partial(grad_kernel, parts, len(experts)), grid=...  11.7 us
  transfers between devices with their start and end apart: 24, of which 11 were waited for; matrix products, arithmetic and copies ran while one was open for 4% of the time, Pallas kernels for 35%

commit v1 on v0

--- a/solution.py
+++ b/solution.py
@@ -11,6 +11,7 @@
 CONTRACT_COLS = (((1,), (1,)), ((), ()))
 ROUTE_ROWS = 8
 VMEM_LIMIT = 24 * 1024 * 1024
+GRAD_VMEM = 56 * 1024 * 1024
 BLOCK_VMEM = 56 * 1024 * 1024
 SMALL_COST = pl.CostEstimate(flops=1000, bytes_accessed=1000, transcendentals=0)
 ANY = pl.BlockSpec(memory_space=pl.ANY)
@@ -229,7 +230,7 @@
         + [pl.BlockSpec((part, tokens), lambda i: (i, 0))] * len(lefts)
         + chosen,
         out_specs=[pl.BlockSpec((len(parts), part, width), lambda i: (0, i, 0))] * len(experts),
-        compiler_params=pltpu.CompilerParams(vmem_limit_bytes=VMEM_LIMIT),
+        compiler_params=pltpu.CompilerParams(vmem_limit_bytes=GRAD_VMEM),
         cost_estimate=SMALL_COST,
         name="grad",
     )(me, *lefts, *[act_all] * len(experts))
@@ -343,13 +344,11 @@
         weights[r + 1] = [gu, hop(down, "expert", 1)]
     if split:
         compute(far, row_of(0) + [(1, 0), (2, 0)], me, False)
-        compute(near, [(1, 1), (2, 1)], me, True)
-        compute(far, [(1, 1), (2, 1)], me, False)
+        compute(near + far, [(1, 1), (2, 1)], me, True)
     else:
         compute(far, row_of(0), me, False)
         for k in (1, 2):
-            compute(near, row_of(k), me, True)
-            compute(far, row_of(k), me, False)
+            compute(near + far, row_of(k), me, True)
     compute(near + far, row_of(3), me, True)
 
     small = lambda v: v.astype(BF16)
@@ -374,7 +373,9 @@
     tick = after(me, [far_down[r] for r in far])
     far_gu = dict(zip(order, grad(tick, order, act_all, xt_all, ct_all, (0, 1))))
     other_gu = [hop(far_gu[r + 1], "expert", 1) for r in far[::2]]
-    other_down, back2 = lax.optimization_barrier((other_down, back2, [far_gu[r] for r in far]))[:2]
+    other_down, back2, back3 = lax.optimization_barrier(
+        (other_down, back2, back3, [far_gu[r] for r in far])
+    )[:3]
     arrived_down, arrived_gu = [], []
     for r, other in zip(far[::2], other_down):
         chip = small(far_down[r].astype(F32) + other.astype(F32))

time: 223 us -> 215 us (0.964)
  waiting for transfers between devices: 98.2 us -> 89.8 us
  Pallas kernels: 80.5 us -> 86.4 us
  local copies, waits for them, and re-layouts: 14.9 us -> 9.51 us
    pallas_call x3, Pallas kernels: 11.7 us -> 21.6 us  [grad(): pl.pallas_call(functools.partial(grad_kernel, parts, len(experts)), grid=...]
    ppermute x24, waiting for transfers between devices: 98.2 us -> 89.8 us  [hop(): lax.ppermute(value, axis, [(i, i ^ step) for i in range(lax.axis_size(axi...]
    unnamed x48 -> x44, local copies, waits for them, and re-layouts: 13.4 us -> 7.97 us
    pallas_call x6 -> x5, Pallas kernels: 64.4 us -> 60.4 us  [block(): pl.pallas_call(functools.partial(block_kernel, tuple(steps), packs, rows,...]
  transfers between devices with their start and end apart: 24 -> 24, of which waited for: 11 -> 11; matrix products, arithmetic and copies ran while one was open for 4% -> 5% of each run, Pallas kernels for 35% -> 39%
where the time goes in v1:
time: 215 us
  waiting for transfers between devices  89.8 us (42%)
  Pallas kernels  86.4 us (40%)
  starting transfers between devices  22.3 us (10%)
  local copies, waits for them, and re-layouts  9.51 us (4%)
  other arithmetic  5.93 us (3%)
    ppermute x24, waiting for transfers between devices, hop(): lax.ppermute(value, axis, [(i, i ^ step) for i in range(lax.axis_size(axi...  89.8 us
    pallas_call x5, Pallas kernels, block(): pl.pallas_call(functools.partial(block_kernel, tuple(steps), packs, rows,...  60.4 us
    ppermute x24, starting transfers between devices, hop(): lax.ppermute(value, axis, [(i, i ^ step) for i in range(lax.axis_size(axi...  22.3 us
    pallas_call x3, Pallas kernels, grad(): pl.pallas_call(functools.partial(grad_kernel, parts, len(experts)), grid=...  21.6 us
    unnamed x44, local copies, waits for them, and re-layouts  7.97 us
    pallas_call x2, Pallas kernels, final_sum(): pl.pallas_call(functools.partial(final_kernel, places, turned, len(parts)...  4.38 us
  transfers between devices with their start and end apart: 24, of which 11 were waited for; matrix products, arithmetic and copies ran while one was open for 5% of the time, Pallas kernels for 39%

profile of v1, /device:TPU:0, one launch (start us, length us, event | category | flops | bytes accessed | tf_op | source)
XLA Modules:
  0.0 214.8 jit_solution(8482365789655059719)
XLA Ops:
  0.6 1.3 constant_dynamic-update-slice_fusion.1
  1.9 0.1 copy-done.15
  2.0 0.1 constant_dynamic-update-slice_fusion.refs_2_.refs_1_
  2.1 0.0 copy-start
  2.1 0.5 collective-permute-start.4
  2.6 2.6 %collective-permute-start.2 = (bf16[2,1536,256]{2,1,0:T(8,128)(2,1)S(1)}, bf16[2,1536,256]{2,1,0:T(8,128)(2,1)}, u32[]{:S(2)}, u32[]{:S(2)}) collective-permute-start(bf16[2,1536,256]{2,1,0:T(8,128)(2,1)S(1)} %constant_dynamic-update-slice_fusion.refs_2_.refs_1_), channel_id=1, source_target_pairs={{0,16},{8,24},{16,0},{24,8},{1,17},{9,25},{17,1},{25,9},{2,18},{10... | collective-permute-start | bytes 4718600 | tf_op jit(solution)/shard_map/ppermute | solution.py:22
  5.2 2.3 %copy.23 = bf16[1,256,1536]{1,2,0:T(8,128)(2,1)} copy(bf16[1,256,1536]{2,1,0:T(8,128)(2,1)} %param.13) | data formatting | bytes 1572864 | tf_op args[6]
  7.5 0.2 collective-permute-start.5
  7.7 2.0 fusion.1.refs_0_
  9.7 1.5 collective-permute-start.3
  11.2 1.6 collective-permute-start
  12.8 0.0 collective-permute-done.5.refs_5_.refs_4_
  12.8 2.6 %collective-permute-start.1 = (bf16[264,1536]{1,0:T(8,128)(2,1)}, bf16[264,1536]{1,0:T(8,128)(2,1)}, u32[]{:S(2)}, u32[]{:S(2)}) collective-permute-start(bf16[264,1536]{1,0:T(8,128)(2,1)} %fusion.1.refs_0_), channel_id=1, source_target_pairs={{0,4},{1,5},{2,6},{3,7},{4,0},{5,1},{6,2},{7,3},{8,12},{9,13},{10,... | collective-permute-start | bytes 2433032 | tf_op jit(solution)/shard_map/ppermute | solution.py:22
  15.3 14.9 %collective-permute-done.3.refs_1_ = bf16[264,1536]{1,0:T(8,128)(2,1)} collective-permute-done((bf16[264,1536]{1,0:T(8,128)(2,1)}, bf16[264,1536]{1,0:T(8,128)(2,1)}, u32[]{:S(2)}, u32[]{:S(2)}) %collective-permute-start.3) | collective-permute-done | bytes 811040 | tf_op jit(solution)/shard_map/ppermute | solution.py:22
  30.3 1.1 copy-done.1
  31.4 8.9 %block.5 = (bf16[264,1536]{1,0:T(8,128)(2,1)}, bf16[264,1536]{1,0:T(8,128)(2,1)}, bf16[4,3,1024,256]{3,2,1,0:T(8,128)(2,1)}, bf16[1536,1024]{1,0:T(8,128)(2,1)}, bf16[1536,1024]{1,0:T(8,128)(2,1)}) custom-call(s32[1]{0:T(128)} %bitcast.me_ref, bf16[264,1536]{1,0:T(8,128)(2,1)} %fusion.1.refs_0_, bf16[264,1536]{1,0:T(8,128)(2,1)} %collective-permute-done.3.refs_1_, ...), custom_call_target="tpu_custom_call" | custom-call | flops 1000 | bytes 1000 | tf_op jit(solution)/shard_map/block/pallas_call | solution.py:183
  40.3 8.5 %collective-permute-done.refs_0_.refs_2_ = bf16[264,1536]{1,0:T(8,128)(2,1)} collective-permute-done((bf16[264,1536]{1,0:T(8,128)(2,1)}, bf16[264,1536]{1,0:T(8,128)(2,1)}, u32[]{:S(2)}, u32[]{:S(2)}) %collective-permute-start) | collective-permute-done | bytes 811040 | tf_op jit(solution)/shard_map/ppermute | solution.py:22
  48.8 2.4 %collective-permute-done.1.refs_1_.refs_3_ = bf16[264,1536]{1,0:T(8,128)(2,1)} collective-permute-done((bf16[264,1536]{1,0:T(8,128)(2,1)}, bf16[264,1536]{1,0:T(8,128)(2,1)}, u32[]{:S(2)}, u32[]{:S(2)}) %collective-permute-start.1) | collective-permute-done | bytes 811040 | tf_op jit(solution)/shard_map/ppermute | solution.py:22
  51.2 0.0 collective-permute-done.2.refs_4_.refs_5_.refs_6_
  51.2 0.0 collective-permute-start.8
  51.2 1.6 pad_maximum_fusion
  52.8 0.6 collective-permute-start.10
  53.4 0.4 collective-permute-start.6
  53.8 0.5 collective-permute-start.7
  54.3 8.8 %block.6 = (bf16[264,1536]{1,0:T(8,128)(2,1)}, bf16[264,1536]{1,0:T(8,128)(2,1)}, bf16[4,3,1024,256]{3,2,1,0:T(8,128)(2,1)}, bf16[1536,1024]{1,0:T(8,128)(2,1)}, bf16[1536,1024]{1,0:T(8,128)(2,1)}) custom-call(s32[1]{0:T(128)} %bitcast.me_ref, ...), custom_call_target="tpu_custom_call", output_to_operand_aliasing={{2}: (7, {}), {3}: (8, {}), {4}: (9, {})} | custom-call | flops 1000 | bytes 1000 | tf_op jit(solution)/shard_map/block/pallas_call | solution.py:183
  63.2 10.0 %collective-permute-done.7.refs_5_.refs_6_.refs_7_ = bf16[1536,256]{1,0:T(8,128)(2,1)S(1)} collective-permute-done((bf16[1536,256]{1,0:T(8,128)(2,1)S(1)}, bf16[1536,256]{1,0:T(8,128)(2,1)S(1)}, u32[]{:S(2)}, u32[]{:S(2)}) %collective-permute-start.7) | collective-permute-done | bytes 786464 | tf_op jit(solution)/shard_map/ppermute | solution.py:22
  73.2 0.6 collective-permute-done.6.refs_0_
  73.8 1.6 collective-permute-start.11
  75.4 2.3 %collective-permute-done.9.refs_7_.refs_8_.refs_9_ = bf16[1536,256]{1,0:T(8,128)(2,1)S(1)} collective-permute-done((bf16[1536,256]{1,0:T(8,128)(2,1)S(1)}, bf16[1536,256]{1,0:T(8,128)(2,1)S(1)}, u32[]{:S(2)}, u32[]{:S(2)}) %collective-permute-start.9) | collective-permute-done | bytes 786464 | tf_op jit(solution)/shard_map/ppermute | solution.py:22
  77.7 0.9 copy-done.5
  78.5 14.6 %block.7 = (bf16[264,1536]{1,0:T(8,128)(2,1)}, bf16[264,1536]{1,0:T(8,128)(2,1)}, bf16[264,1536]{1,0:T(8,128)(2,1)}, bf16[264,1536]{1,0:T(8,128)(2,1)}, bf16[4,3,1024,256]{3,2,1,0:T(8,128)(2,1)}) custom-call(s32[1]{0:T(128)} %bitcast.me_ref, bf16[264,1536]{1,0:T(8,128)(2,1)} %fusion.1.refs_0_, ...), custom_call_target="tpu_custom_call", output_to_operand_aliasing={{4}: (13, {})} | custom-call | flops 1000 | bytes 1000 | tf_op jit(solution)/shard_map/block/pallas_call | solution.py:183
  93.2 1.2 copy-done.7
  94.4 13.9 %block.8 = (bf16[264,1536]{1,0:T(8,128)(2,1)}, bf16[264,1536]{1,0:T(8,128)(2,1)}, bf16[4,3,1024,256]{3,2,1,0:T(8,128)(2,1)}, bf16[1536,1024]{1,0:T(8,128)(2,1)}, bf16[1536,1024]{1,0:T(8,128)(2,1)}) custom-call(s32[1]{0:T(128)} %bitcast.me_ref, bf16[2,264,1536]{2,1,0:T(8,128)(2,1)} %copy-done.7, ...), custom_call_target="tpu_custom_call", output_to_operand_aliasing={{2}: (10, {}), {3}: (11, {}), {4}: (12, {})} | custom-call | flops 1000 | bytes 1000 | tf_op jit(solution)/shard_map/block/pallas_call | solution.py:183
  108.4 0.6 collective-permute-start.13
  108.9 1.0 copy-done.10
  109.9 14.2 %block.9 = (bf16[264,1536]{1,0:T(8,128)(2,1)}, bf16[264,1536]{1,0:T(8,128)(2,1)}, bf16[4,3,1024,256]{3,2,1,0:T(8,128)(2,1)}, bf16[1536,1024]{1,0:T(8,128)(2,1)}, bf16[1536,1024]{1,0:T(8,128)(2,1)}) custom-call(s32[1]{0:T(128)} %bitcast.me_ref, bf16[264,1536]{1,0:T(8,128)(2,1)} %copy-done.9, ...), custom_call_target="tpu_custom_call", output_to_operand_aliasing={{2}: (11, {}), {3}: (12, {}), {4}: (13, {})} | custom-call | flops 1000 | bytes 1000 | tf_op jit(solution)/shard_map/block/pallas_call | solution.py:183
  124.1 1.6 collective-permute-start.14
  125.7 5.1 %grad.3 = (bf16[1,1536,256]{2,1,0:T(8,128)(2,1)}, bf16[1,1536,256]{2,1,0:T(8,128)(2,1)}) custom-call(s32[1]{0:T(128)} %bitcast.me_ref, bf16[1536,1024]{1,0:T(8,128)(2,1)} %get-tuple-element.107.refs_0_.refs_1_, bf16[4,3,1024,256]{3,2,1,0:T(8,128)(2,1)} %get-tuple-element.105.refs_1_.refs_2_.refs_3_, ...), custom_call_target="tpu_custom_call" | custom-call | flops 1000 | bytes 1000 | tf_op jit(solution)/shard_map/grad/pallas_call | solution.py:225
  130.9 7.0 %grad.4 = (bf16[2,1536,256]{2,1,0:T(8,128)(2,1)}, bf16[2,1536,256]{2,1,0:T(8,128)(2,1)}) custom-call(s32[1]{0:T(128)} %bitcast.me_ref, bf16[1536,1024]{1,0:T(8,128)(2,1)} %get-tuple-element.113.refs_0_, bf16[4,3,1024,256]{3,2,1,0:T(8,128)(2,1)} %get-tuple-element.105.refs_1_.refs_2_.refs_3_, bf16[4,3,1024,256]{3,2,1,0:T(8,128)(2,1)} %get-tuple-element.105.refs_1_.refs_2_.refs_3_), custom_call_target="tpu_custom_call" | custom-call | flops 1000 | bytes 1000 | tf_op jit(solution)/shard_map/grad/pallas_call | solution.py:225
  137.9 0.5 collective-permute-start.18
  138.4 7.7 %collective-permute-done.14 = bf16[264,1536]{1,0:T(8,128)(2,1)S(1)} collective-permute-done((bf16[264,1536]{1,0:T(8,128)(2,1)}, bf16[264,1536]{1,0:T(8,128)(2,1)S(1)}, u32[]{:S(2)}, u32[]{:S(2)}) %collective-permute-start.14) | collective-permute-done | bytes 811040 | tf_op jit(solution)/shard_map/ppermute | solution.py:22
  146.1 0.2 add_convert_fusion.5
  146.4 0.6 collective-permute-start.16
  146.9 0.2 add_convert_fusion.4
  147.2 1.1 collective-permute-start.15
  148.3 0.5 collective-permute-start.17
  148.8 9.4 %grad.5 = (bf16[3,1536,256]{2,1,0:T(8,128)(2,1)}, bf16[3,1536,256]{2,1,0:T(8,128)(2,1)}) custom-call(s32[1]{0:T(128)} %bitcast.me_ref, bf16[1536,1024]{1,0:T(8,128)(2,1)} %get-tuple-element.113.refs_0_, bf16[1536,1024]{1,0:T(8,128)(2,1)} %get-tuple-element.107.refs_0_.refs_1_, bf16[4,3,1024,256]{3,2,1,0:T(8,128)(2,1)} %get-tuple-element.105.refs_1_.refs_2_.refs_3_, ...), custom_call_target="tpu_custom_call" | custom-call | flops 1000 | bytes 1000 | tf_op jit(solution)/shard_map/grad/pallas_call | solution.py:225
  158.2 8.2 %collective-permute-done.17.refs_1_ = bf16[1,1536,256]{2,1,0:T(8,128)(2,1)S(1)} collective-permute-done((bf16[1,1536,256]{2,1,0:T(8,128)(2,1)S(1)}, bf16[1,1536,256]{2,1,0:T(8,128)(2,1)S(1)}, u32[]{:S(2)}, u32[]{:S(2)}) %collective-permute-start.17) | collective-permute-done | bytes 786464 | tf_op jit(solution)/shard_map/ppermute | solution.py:22
  166.5 1.6 collective-permute-start.19
  168.1 0.2 add_convert_fusion.3
  168.3 1.1 collective-permute-start.20
  169.4 0.3 add_convert_fusion.2
  169.7 2.1 collective-permute-start.21
  171.8 0.4 add_convert_fusion.1
  172.2 0.6 collective-permute-start.23
  172.8 14.2 %collective-permute-done.19 = bf16[264,1536]{1,0:T(8,128)(2,1)S(1)} collective-permute-done((bf16[264,1536]{1,0:T(8,128)(2,1)S(1)}, bf16[264,1536]{1,0:T(8,128)(2,1)S(1)}, u32[]{:S(2)}, u32[]{:S(2)}) %collective-permute-start.19) | collective-permute-done | bytes 811040 | tf_op jit(solution)/shard_map/ppermute | solution.py:22
  187.0 18.4 %collective-permute-done.20 = bf16[264,1536]{1,0:T(8,128)(2,1)S(1)} collective-permute-done((bf16[264,1536]{1,0:T(8,128)(2,1)S(1)}, bf16[264,1536]{1,0:T(8,128)(2,1)S(1)}, u32[]{:S(2)}, u32[]{:S(2)}) %collective-permute-start.20) | collective-permute-done | bytes 811040 | tf_op jit(solution)/shard_map/ppermute | solution.py:22
  205.4 2.5 %collective-permute-done.21 = bf16[264,1536]{1,0:T(8,128)(2,1)S(1)} collective-permute-done((bf16[264,1536]{1,0:T(8,128)(2,1)S(1)}, bf16[264,1536]{1,0:T(8,128)(2,1)S(1)}, u32[]{:S(2)}, u32[]{:S(2)}) %collective-permute-start.21) | collective-permute-done | bytes 811040 | tf_op jit(solution)/shard_map/ppermute | solution.py:22
  207.9 0.4 fusion.3
  208.4 0.6 slice_bitcast_fusion
  208.9 0.9 fusion.4
  209.8 0.5 add_convert_fusion.refs_0_
  210.4 2.1 final.3
  212.5 2.2 %final.2 = (f32[1,1536,256]{2,1,0:T(8,128)}, f32[1,1536,256]{2,1,0:T(8,128)}) custom-call(bf16[3,1536,256]{2,1,0:T(8,128)(2,1)S(1)} %add_convert_fusion.refs_0_, bf16[2,1536,256]{2,1,0:T(8,128)(2,1)S(1)} %collective-permute-done.23.refs_1_), custom_call_target="tpu_custom_call" | custom-call | flops 1000 | bytes 1000 | tf_op jit(solution)/shard_map/final/pallas_call | solution.py:255
  (53 shorter events, 0.1 us)
Async XLA Ops:
  0.6 1.4 copy-start.15
  2.0 5.6 %copy-start.20 = (s32[128,2]{0,1:T(2,128)S(1)}, s32[128,2]{0,1:T(2,128)}, u32[]{:S(2)}) copy-start(s32[128,2]{0,1:T(2,128)} %param.9) | copy-start | bytes 3076
  2.0 5.6 %copy-start.18 = (f32[128,2]{0,1:T(2,128)S(1)}, f32[128,2]{0,1:T(2,128)}, u32[]{:S(2)}) copy-start(f32[128,2]{0,1:T(2,128)} %param.8) | copy-start | bytes 3076
  2.0 5.7 %copy-start.17 = (bf16[128,1536]{1,0:T(8,128)(2,1)S(1)}, bf16[128,1536]{1,0:T(8,128)(2,1)}, u32[]{:S(2)}) copy-start(bf16[128,1536]{1,0:T(8,128)(2,1)} %param.10) | copy-start | bytes 1179652
  2.1 28.2 %copy-start = (bf16[2,1536,256]{2,1,0:T(8,128)(2,1)}, bf16[2,1536,256]{2,1,0:T(8,128)(2,1)S(1)}, u32[]{:S(2)}) copy-start(bf16[2,1536,256]{2,1,0:T(8,128)(2,1)S(1)} %constant_dynamic-update-slice_fusion.refs_2_.refs_1_) | copy-start | bytes 4718596
  2.1 28.2 %collective-permute-start.4 = (bf16[2,1536,256]{2,1,0:T(8,128)(2,1)S(1)}, bf16[2,1536,256]{2,1,0:T(8,128)(2,1)S(1)}, u32[]{:S(2)}, u32[]{:S(2)}) collective-permute-start(bf16[2,1536,256]{2,1,0:T(8,128)(2,1)S(1)} %constant_dynamic-update-slice_fusion.refs_2_.refs_1_), channel_id=1, source_target_pairs={{0,8},{8,0},{16,24},{24,16},{1,9},{9,1},{17,25},{25,17},{2,10},{10... | collective-permute-start | bytes 4718600 | tf_op jit(solution)/shard_map/ppermute | solution.py:22
  2.6 48.6 %collective-permute-start.2 = (bf16[2,1536,256]{2,1,0:T(8,128)(2,1)S(1)}, bf16[2,1536,256]{2,1,0:T(8,128)(2,1)}, u32[]{:S(2)}, u32[]{:S(2)}) collective-permute-start(bf16[2,1536,256]{2,1,0:T(8,128)(2,1)S(1)} %constant_dynamic-update-slice_fusion.refs_2_.refs_1_), channel_id=1, source_target_pairs={{0,16},{8,24},{16,0},{24,8},{1,17},{9,25},{17,1},{25,9},{2,18},{10... | collective-permute-start | bytes 4718600 | tf_op jit(solution)/shard_map/ppermute | solution.py:22
  7.5 5.3 %collective-permute-start.5 = (bf16[1536,256]{1,0:T(8,128)(2,1)}, bf16[1536,256]{1,0:T(8,128)(2,1)}, u32[]{:S(2)}, u32[]{:S(2)}) collective-permute-start(bf16[1536,256]{1,0:T(8,128)(2,1)} %bitcast.10), channel_id=1, source_target_pairs={{0,8},{8,0},{16,24},{24,16},{1,9},{9,1},{17,25},{25,17},{2,10},{10... | collective-permute-start | bytes 2359304 | tf_op jit(solution)/shard_map/ppermute | solution.py:22
  9.7 20.6 %collective-permute-start.3 = (bf16[264,1536]{1,0:T(8,128)(2,1)}, bf16[264,1536]{1,0:T(8,128)(2,1)}, u32[]{:S(2)}, u32[]{:S(2)}) collective-permute-start(bf16[264,1536]{1,0:T(8,128)(2,1)} %fusion.1.refs_0_), channel_id=1, source_target_pairs={{0,1},{1,0},{2,3},{3,2},{4,5},{5,4},{6,7},{7,6},{8,9},{9,8},{10,11... | collective-permute-start | bytes 2433032 | tf_op jit(solution)/shard_map/ppermute | solution.py:22
  11.2 37.6 %collective-permute-start = (bf16[264,1536]{1,0:T(8,128)(2,1)}, bf16[264,1536]{1,0:T(8,128)(2,1)}, u32[]{:S(2)}, u32[]{:S(2)}) collective-permute-start(bf16[264,1536]{1,0:T(8,128)(2,1)} %fusion.1.refs_0_), channel_id=1, source_target_pairs={{0,2},{1,3},{2,0},{3,1},{4,6},{5,7},{6,4},{7,5},{8,10},{9,11},{10,... | collective-permute-start | bytes 2433032 | tf_op jit(solution)/shard_map/ppermute | solution.py:22
  12.8 38.4 %collective-permute-start.1 = (bf16[264,1536]{1,0:T(8,128)(2,1)}, bf16[264,1536]{1,0:T(8,128)(2,1)}, u32[]{:S(2)}, u32[]{:S(2)}) collective-permute-start(bf16[264,1536]{1,0:T(8,128)(2,1)} %fusion.1.refs_0_), channel_id=1, source_target_pairs={{0,4},{1,5},{2,6},{3,7},{4,0},{5,1},{6,2},{7,3},{8,12},{9,13},{10,... | collective-permute-start | bytes 2433032 | tf_op jit(solution)/shard_map/ppermute | solution.py:22
  30.3 1.1 copy-start.1
  51.2 22.6 %collective-permute-start.8 = (bf16[2,1536,256]{2,1,0:T(8,128)(2,1)}, bf16[2,1536,256]{2,1,0:T(8,128)(2,1)S(1)}, u32[]{:S(2)}, u32[]{:S(2)}) collective-permute-start(bf16[2,1536,256]{2,1,0:T(8,128)(2,1)} %collective-permute-done.2.refs_4_.refs_5_.refs_6_), channel_id=1, source_target_pairs={{0,8},{8,0},{16,24},{24,16},{1,9},{9,1},{17,25},{25,17},{2,10},{10... | collective-permute-start | bytes 4718600 | tf_op jit(solution)/shard_map/ppermute | solution.py:22
  51.2 2.6 %copy-start.2 = (bf16[1,256,1536]{1,2,0:T(8,128)(2,1)S(1)}, bf16[1,256,1536]{1,2,0:T(8,128)(2,1)}, u32[]{:S(2)}) copy-start(bf16[1,256,1536]{1,2,0:T(8,128)(2,1)} %copy.23) | copy-start | bytes 2359300
  52.8 40.4 %collective-permute-start.10 = (bf16[2,264,1536]{2,1,0:T(8,128)(2,1)S(1)}, bf16[2,264,1536]{2,1,0:T(8,128)(2,1)S(1)}, u32[]{:S(2)}, u32[]{:S(2)}) collective-permute-start(bf16[2,264,1536]{2,1,0:T(8,128)(2,1)S(1)} %pad_maximum_fusion), channel_id=1, source_target_pairs={{0,1},{1,0},{2,3},{3,2},{4,5},{5,4},{6,7},{7,6},{8,9},{9,8},{10,11... | collective-permute-start | bytes 4866056 | tf_op jit(solution)/shard_map/ppermute | solution.py:22
  53.4 20.4 %collective-permute-start.6 = (bf16[264,1536]{1,0:T(8,128)(2,1)}, bf16[264,1536]{1,0:T(8,128)(2,1)S(1)}, u32[]{:S(2)}, u32[]{:S(2)}) collective-permute-start(bf16[264,1536]{1,0:T(8,128)(2,1)} %collective-permute-done.1.refs_1_.refs_3_), channel_id=1, source_target_pairs={{0,2},{1,3},{2,0},{3,1},{4,6},{5,7},{6,4},{7,5},{8,10},{9,11},{10,... | collective-permute-start | bytes 2433032 | tf_op jit(solution)/shard_map/ppermute | solution.py:22
  53.8 19.4 %collective-permute-start.7 = (bf16[1536,256]{1,0:T(8,128)(2,1)S(1)}, bf16[1536,256]{1,0:T(8,128)(2,1)S(1)}, u32[]{:S(2)}, u32[]{:S(2)}) collective-permute-start(bf16[1536,256]{1,0:T(8,128)(2,1)S(1)} %bitcast.15), channel_id=1, source_target_pairs={{0,16},{8,24},{16,0},{24,8},{1,17},{9,25},{17,1},{25,9},{2,18},{10... | collective-permute-start | bytes 2359304 | tf_op jit(solution)/shard_map/ppermute | solution.py:22
  73.2 4.5 %copy-start.4 = (bf16[1536,256]{1,0:T(8,128)(2,1)}, bf16[1536,256]{1,0:T(8,128)(2,1)S(1)}, u32[]{:S(2)}) copy-start(bf16[1536,256]{1,0:T(8,128)(2,1)S(1)} %collective-permute-done.7.refs_5_.refs_6_.refs_7_) | copy-start | bytes 2359300
  73.8 19.4 %copy-start.9 = (bf16[264,1536]{1,0:T(8,128)(2,1)}, bf16[264,1536]{1,0:T(8,128)(2,1)S(1)}, u32[]{:S(2)}) copy-start(bf16[264,1536]{1,0:T(8,128)(2,1)S(1)} %collective-permute-done.6.refs_0_) | copy-start | bytes 2433028
  73.8 3.9 %copy-start.3 = (bf16[2,1536,256]{2,1,0:T(8,128)(2,1)}, bf16[2,1536,256]{2,1,0:T(8,128)(2,1)S(1)}, u32[]{:S(2)}) copy-start(bf16[2,1536,256]{2,1,0:T(8,128)(2,1)S(1)} %collective-permute-done.8.refs_6_.refs_7_.refs_8_) | copy-start | bytes 4718596
  73.8 35.2 %collective-permute-start.11 = (bf16[264,1536]{1,0:T(8,128)(2,1)S(1)}, bf16[264,1536]{1,0:T(8,128)(2,1)S(1)}, u32[]{:S(2)}, u32[]{:S(2)}) collective-permute-start(bf16[264,1536]{1,0:T(8,128)(2,1)S(1)} %collective-permute-done.6.refs_0_), channel_id=1, source_target_pairs={{0,1},{1,0},{2,3},{3,2},{4,5},{5,4},{6,7},{7,6},{8,9},{9,8},{10,11... | collective-permute-start | bytes 2433032 | tf_op jit(solution)/shard_map/ppermute | solution.py:22
  75.4 2.3 %collective-permute-start.9 = (bf16[1536,256]{1,0:T(8,128)(2,1)S(1)}, bf16[1536,256]{1,0:T(8,128)(2,1)S(1)}, u32[]{:S(2)}, u32[]{:S(2)}) collective-permute-start(bf16[1536,256]{1,0:T(8,128)(2,1)S(1)} %collective-permute-done.7.refs_5_.refs_6_.refs_7_), channel_id=1, source_target_pairs={{0,8},{8,0},{16,24},{24,16},{1,9},{9,1},{17,25},{25,17},{2,10},{10... | collective-permute-start | bytes 2359304 | tf_op jit(solution)/shard_map/ppermute | solution.py:22
  77.6 0.9 copy-start.5
  93.2 1.2 copy-start.7
  108.4 30.0 %collective-permute-start.13 = (bf16[264,1536]{1,0:T(8,128)(2,1)}, bf16[264,1536]{1,0:T(8,128)(2,1)S(1)}, u32[]{:S(2)}, u32[]{:S(2)}) collective-permute-start(bf16[264,1536]{1,0:T(8,128)(2,1)} %get-tuple-element.109), channel_id=1, source_target_pairs={{0,1},{1,0},{2,3},{3,2},{4,5},{5,4},{6,7},{7,6},{8,9},{9,8},{10,11... | collective-permute-start | bytes 2433032 | tf_op jit(solution)/shard_map/ppermute | solution.py:22
  108.9 1.0 copy-start.10
  124.1 22.0 %collective-permute-start.14 = (bf16[264,1536]{1,0:T(8,128)(2,1)}, bf16[264,1536]{1,0:T(8,128)(2,1)S(1)}, u32[]{:S(2)}, u32[]{:S(2)}) collective-permute-start(bf16[264,1536]{1,0:T(8,128)(2,1)} %get-tuple-element.110), channel_id=1, source_target_pairs={{0,1},{1,0},{2,3},{3,2},{4,5},{5,4},{6,7},{7,6},{8,9},{9,8},{10,11... | collective-permute-start | bytes 2433032 | tf_op jit(solution)/shard_map/ppermute | solution.py:22
  130.8 7.5 %collective-permute-start.12 = (bf16[1,1536,256]{2,1,0:T(8,128)(2,1)}, bf16[1,1536,256]{2,1,0:T(8,128)(2,1)S(1)}, u32[]{:S(2)}, u32[]{:S(2)}) collective-permute-start(bf16[1,1536,256]{2,1,0:T(8,128)(2,1)} %get-tuple-element.108), channel_id=1, source_target_pairs={{0,8},{8,0},{16,24},{24,16},{1,9},{9,1},{17,25},{25,17},{2,10},{10... | collective-permute-start | bytes 2359304 | tf_op jit(solution)/shard_map/ppermute | solution.py:22
  130.8 15.3 %copy-start.16 = (bf16[1,1536,256]{2,1,0:T(8,128)(2,1)S(1)}, bf16[1,1536,256]{2,1,0:T(8,128)(2,1)}, u32[]{:S(2)}) copy-start(bf16[1,1536,256]{2,1,0:T(8,128)(2,1)} %get-tuple-element.111) | copy-start | bytes 2359300
  137.9 9.1 %copy-start.13 = (bf16[264,1536]{1,0:T(8,128)(2,1)S(1)}, bf16[264,1536]{1,0:T(8,128)(2,1)}, u32[]{:S(2)}) copy-start(bf16[264,1536]{1,0:T(8,128)(2,1)} %get-tuple-element.104) | copy-start | bytes 2433028
  137.9 20.4 %collective-permute-start.18 = (bf16[2,1536,256]{2,1,0:T(8,128)(2,1)}, bf16[2,1536,256]{2,1,0:T(8,128)(2,1)S(1)}, u32[]{:S(2)}, u32[]{:S(2)}) collective-permute-start(bf16[2,1536,256]{2,1,0:T(8,128)(2,1)} %get-tuple-element.115), channel_id=1, source_target_pairs={{0,8},{8,0},{16,24},{24,16},{1,9},{9,1},{17,25},{25,17},{2,10},{10... | collective-permute-start | bytes 4718600 | tf_op jit(solution)/shard_map/ppermute | solution.py:22
  146.4 20.1 %collective-permute-start.16 = (bf16[264,1536]{1,0:T(8,128)(2,1)}, bf16[264,1536]{1,0:T(8,128)(2,1)S(1)}, u32[]{:S(2)}, u32[]{:S(2)}) collective-permute-start(bf16[264,1536]{1,0:T(8,128)(2,1)} %get-tuple-element.121), channel_id=1, source_target_pairs={{0,1},{1,0},{2,3},{3,2},{4,5},{5,4},{6,7},{7,6},{8,9},{9,8},{10,11... | collective-permute-start | bytes 2433032 | tf_op jit(solution)/shard_map/ppermute | solution.py:22
  147.2 19.3 %copy-start.19 = (bf16[264,1536]{1,0:T(8,128)(2,1)S(1)}, bf16[264,1536]{1,0:T(8,128)(2,1)}, u32[]{:S(2)}) copy-start(bf16[264,1536]{1,0:T(8,128)(2,1)} %get-tuple-element.126) | copy-start | bytes 2433028
  147.2 20.9 %copy-start.12 = (bf16[264,1536]{1,0:T(8,128)(2,1)S(1)}, bf16[264,1536]{1,0:T(8,128)(2,1)}, u32[]{:S(2)}) copy-start(bf16[264,1536]{1,0:T(8,128)(2,1)} %get-tuple-element.127) | copy-start | bytes 2433028
  147.2 19.3 %collective-permute-start.15 = (bf16[264,1536]{1,0:T(8,128)(2,1)S(1)}, bf16[264,1536]{1,0:T(8,128)(2,1)S(1)}, u32[]{:S(2)}, u32[]{:S(2)}) collective-permute-start(bf16[264,1536]{1,0:T(8,128)(2,1)S(1)} %add_convert_fusion.4), channel_id=1, source_target_pairs={{0,2},{1,3},{2,0},{3,1},{4,6},{5,7},{6,4},{7,5},{8,10},{9,11},{10,... | collective-permute-start | bytes 2433032 | tf_op jit(solution)/shard_map/ppermute | solution.py:22
  148.3 18.2 %collective-permute-start.17 = (bf16[1,1536,256]{2,1,0:T(8,128)(2,1)S(1)}, bf16[1,1536,256]{2,1,0:T(8,128)(2,1)S(1)}, u32[]{:S(2)}, u32[]{:S(2)}) collective-permute-start(bf16[1,1536,256]{2,1,0:T(8,128)(2,1)S(1)} %add_convert_fusion.5), channel_id=1, source_target_pairs={{0,16},{8,24},{16,0},{24,8},{1,17},{9,25},{17,1},{25,9},{2,18},{10... | collective-permute-start | bytes 2359304 | tf_op jit(solution)/shard_map/ppermute | solution.py:22
  158.2 11.1 %copy-start.11 = (bf16[264,1536]{1,0:T(8,128)(2,1)S(1)}, bf16[264,1536]{1,0:T(8,128)(2,1)}, u32[]{:S(2)}) copy-start(bf16[264,1536]{1,0:T(8,128)(2,1)} %get-tuple-element.128) | copy-start | bytes 2433028
  166.5 43.4 %collective-permute-start.22 = (bf16[3,1536,256]{2,1,0:T(8,128)(2,1)}, bf16[3,1536,256]{2,1,0:T(8,128)(2,1)S(1)}, u32[]{:S(2)}, u32[]{:S(2)}) collective-permute-start(bf16[3,1536,256]{2,1,0:T(8,128)(2,1)} %get-tuple-element.131), channel_id=1, source_target_pairs={{0,8},{8,0},{16,24},{24,16},{1,9},{9,1},{17,25},{25,17},{2,10},{10... | collective-permute-start | bytes 7077896 | tf_op jit(solution)/shard_map/ppermute | solution.py:22
  166.5 20.5 %collective-permute-start.19 = (bf16[264,1536]{1,0:T(8,128)(2,1)S(1)}, bf16[264,1536]{1,0:T(8,128)(2,1)S(1)}, u32[]{:S(2)}, u32[]{:S(2)}) collective-permute-start(bf16[264,1536]{1,0:T(8,128)(2,1)S(1)} %copy-done.19), channel_id=1, source_target_pairs={{0,1},{1,0},{2,3},{3,2},{4,5},{5,4},{6,7},{7,6},{8,9},{9,8},{10,11... | collective-permute-start | bytes 2433032 | tf_op jit(solution)/shard_map/ppermute | solution.py:22
  168.3 37.1 %collective-permute-start.20 = (bf16[264,1536]{1,0:T(8,128)(2,1)S(1)}, bf16[264,1536]{1,0:T(8,128)(2,1)S(1)}, u32[]{:S(2)}, u32[]{:S(2)}) collective-permute-start(bf16[264,1536]{1,0:T(8,128)(2,1)S(1)} %add_convert_fusion.3), channel_id=1, source_target_pairs={{0,2},{1,3},{2,0},{3,1},{4,6},{5,7},{6,4},{7,5},{8,10},{9,11},{10,... | collective-permute-start | bytes 2433032 | tf_op jit(solution)/shard_map/ppermute | solution.py:22
  169.4 2.4 %copy-start.8 = (bf16[2,1536,256]{2,1,0:T(8,128)(2,1)S(1)}, bf16[2,1536,256]{2,1,0:T(8,128)(2,1)}, u32[]{:S(2)}) copy-start(bf16[2,1536,256]{2,1,0:T(8,128)(2,1)} %get-tuple-element.114) | copy-start | bytes 4718596
  169.7 38.3 %copy-start.14 = (bf16[264,1536]{1,0:T(8,128)(2,1)S(1)}, bf16[264,1536]{1,0:T(8,128)(2,1)}, u32[]{:S(2)}) copy-start(bf16[264,1536]{1,0:T(8,128)(2,1)} %get-tuple-element.93) | copy-start | bytes 2433028
  169.7 38.2 %collective-permute-start.21 = (bf16[264,1536]{1,0:T(8,128)(2,1)S(1)}, bf16[264,1536]{1,0:T(8,128)(2,1)S(1)}, u32[]{:S(2)}, u32[]{:S(2)}) collective-permute-start(bf16[264,1536]{1,0:T(8,128)(2,1)S(1)} %add_convert_fusion.2), channel_id=1, source_target_pairs={{0,4},{1,5},{2,6},{3,7},{4,0},{5,1},{6,2},{7,3},{8,12},{9,13},{10,... | collective-permute-start | bytes 2433032 | tf_op jit(solution)/shard_map/ppermute | solution.py:22
  172.2 40.3 %collective-permute-start.23 = (bf16[2,1536,256]{2,1,0:T(8,128)(2,1)S(1)}, bf16[2,1536,256]{2,1,0:T(8,128)(2,1)S(1)}, u32[]{:S(2)}, u32[]{:S(2)}) collective-permute-start(bf16[2,1536,256]{2,1,0:T(8,128)(2,1)S(1)} %add_convert_fusion.1), channel_id=1, source_target_pairs={{0,16},{8,24},{16,0},{24,8},{1,17},{9,25},{17,1},{25,9},{2,18},{10... | collective-permute-start | bytes 4718600 | tf_op jit(solution)/shard_map/ppermute | solution.py:22
  207.9 1.9 copy-start.6

commit v2 on v1

--- a/solution.py
+++ b/solution.py
@@ -62,18 +62,27 @@
     width = hp_ref.shape[1] // len(steps)
     at = lambda n: slice(n * width, (n + 1) * width)
     w_copies = []
-    for i, (gu, down) in enumerate(weights):
-        targets = (gu_ref.at[:, at(2 * i)], gu_ref.at[:, at(2 * i + 1)], down_ref.at[:, at(i)])
+    half = columns // 2
+    for i, (five, one) in enumerate(weights):
+        targets = [gu_ref.at[:, at(2 * i)], gu_ref.at[:, at(2 * i + 1)], down_ref.at[:, at(i)]]
+        sources = [five.at[n] for n in range(5)] + [one.at[0]]
         w_copies.append(
             [
-                pltpu.make_async_copy(w, target, w_sem.at[i, m])
-                for m, (w, target) in enumerate(zip((gu.at[0], gu.at[1], down), targets))
+                [
+                    pltpu.make_async_copy(
+                        sources[2 * m + n],
+                        targets[m].at[n * half : (n + 1) * half, :],
+                        w_sem.at[i, 2 * m + n],
+                    )
+                    for n in range(2)
+                ]
+                for m in range(3)
             ]
         )
     acc_copies = [
         pltpu.make_async_copy(a, r, acc_sem.at[j]) for j, (a, r) in enumerate(zip(accs, acc_refs))
     ]
-    for copy in [c for group in w_copies for c in group] + acc_copies:
+    for copy in [c for group in w_copies for two in group for c in two] + acc_copies:
         copy.start()
     for j, pay in enumerate(pays):
         x_ref[j * rows : (j + 1) * rows, :] = pay[0:rows, :]
@@ -105,11 +114,14 @@
         e = (me_ref[0] ^ step).astype(F32)
         prob = jnp.where(stand[:, 4:5] == e, stand[:, 0:1] + stand[:, 2:3], 0.0)
         prob = prob + jnp.where(stand[:, 5:6] == e, stand[:, 1:2] + stand[:, 3:4], 0.0)
-        w_copies[i][0].wait()
+        for copy in w_copies[i][0]:
+            copy.wait()
         pre_gate = nn(x_ref[...], gu_ref[:, at(2 * i)])
-        w_copies[i][1].wait()
+        for copy in w_copies[i][1]:
+            copy.wait()
         pre_up = nn(x_ref[...], gu_ref[:, at(2 * i + 1)])
-        w_copies[i][2].wait()
+        for copy in w_copies[i][2]:
+            copy.wait()
         d_raw = nn(c_ref[...], down_ref[:, at(i)])
         sig = jax.nn.sigmoid(pre_gate)
         silu = pre_gate * sig
@@ -136,13 +148,13 @@
                 act_copies.append(copy)
     for copy in acc_copies:
         copy.wait()
-    for half, (left, right) in enumerate(((hp_ref, down_ref), (dgu_ref, gu_ref))):
+    for side, (left, right) in enumerate(((hp_ref, down_ref), (dgu_ref, gu_ref))):
         value = nt(left[...], right[...])
         for j, out in enumerate(outs):
             part = value[j * rows : (j + 1) * rows]
             if has_acc:
-                part = part + acc_refs[j][half * rows : (half + 1) * rows, :].astype(F32)
-            out[half * rows : (half + 1) * rows, :] = part.astype(out.dtype)
+                part = part + acc_refs[j][side * rows : (side + 1) * rows, :].astype(F32)
+            out[side * rows : (side + 1) * rows, :] = part.astype(out.dtype)
     for j, out in enumerate(outs):
         pair = jnp.concatenate(
             [g[:, j * rows : (j + 1) * rows] for g in gates]
@@ -162,7 +174,7 @@
     packs = tuple(p[1] if isinstance(p, tuple) else None for p in pays)
     pays = [p[0] if isinstance(p, tuple) else p for p in pays]
     height, columns = pays[0].shape[-2:]
-    width = weights[0][1].shape[1]
+    width = weights[0][1].shape[2]
     total = shards * rows
     outs = [jax.ShapeDtypeStruct((height, columns), BF16)] * shards
     filled = [jax.ShapeDtypeStruct((experts, 3, tokens, width), BF16)]
@@ -179,7 +191,7 @@
     if accs:
         scratch += [pltpu.VMEM(a.shape, BF16) for a in accs]
     dma = pltpu.SemaphoreType.DMA
-    scratch += [dma((count, 3)), dma((count, 3, shards)), dma((2, shards)), dma((shards,))]
+    scratch += [dma((count, 6)), dma((count, 3, shards)), dma((2, shards)), dma((shards,))]
     res = pl.pallas_call(
         functools.partial(
             block_kernel, tuple(steps), packs, rows, tuple(places), bool(accs), with_t, len(old)
@@ -279,7 +291,12 @@
     beside = lambda v: [hop(v, "fsdp", j) for j in range(1, inner)]
     near, far = [0, 1], list(range(2, experts))
     size = dict(experts=experts, tokens=outer * inner * rows, rows=rows)
-    own_w = [jnp.stack([gate_weight[0], up_weight[0]]), down_weight[0].T]
+    halves = lambda w: w.reshape(2, columns // 2, -1)
+    turned = halves(after(down_weight[0], own_pay).T)
+    own_w = [
+        jnp.concatenate([halves(gate_weight[0]), halves(up_weight[0]), turned[:1]]),
+        turned[1:],
+    ]
     weights = {r: [None] * 2 for r in range(experts)}
     weights[0] = own_w
     pays, keep, done, shared = {}, {}, {}, None
@@ -335,18 +352,21 @@
         compute(near, [(1, 0), (2, 0)], me, True)
     downs = [weights[r][1] for r in far[::2]]
     gus = [weights[r + 1][0] for r in far[::2]]
-    third, downs, gus, shared = lax.optimization_barrier((third, downs, gus, shared))
-
-    for j, p in enumerate([third] + beside(third)):
-        pays[3, j] = p
+    downs, gus, shared = lax.optimization_barrier((downs, gus, shared))
     for r, gu, down in zip(far[::2], gus, downs):
         weights[r][1] = down
         weights[r + 1] = [gu, hop(down, "expert", 1)]
+
     if split:
         compute(far, row_of(0) + [(1, 0), (2, 0)], me, False)
+    else:
+        compute(far, row_of(0), me, False)
+    third, shared = lax.optimization_barrier((third, shared))
+    for j, p in enumerate([third] + beside(third)):
+        pays[3, j] = p
+    if split:
         compute(near + far, [(1, 1), (2, 1)], me, True)
     else:
-        compute(far, row_of(0), me, False)
         for k in (1, 2):
             compute(near + far, row_of(k), me, True)
     compute(near + far, row_of(3), me, True)
@@ -384,23 +404,25 @@
     sum3 = small(join(3, after(back3, chip)))
     up3 = hop(sum3, "fsdp", inner)
     near_grads = grad(after(me, sum3), near[::-1], act_all, xt_all, ct_all, (0, 1, 2))
-    up3, back1, arrived_down, other_gu, near_grads = lax.optimization_barrier(
-        (up3, back1, arrived_down, other_gu, near_grads)
+    other_gu = after(other_gu, near_grads)
+    chips = [
+        small(far_gu[r].astype(F32) + other.astype(F32)) for r, other in zip(far[::2], other_gu)
+    ]
+    up3, back1, arrived_down, chips, near_grads = lax.optimization_barrier(
+        (up3, back1, arrived_down, chips, near_grads)
     )
+    arrived_gu = [hop(chip, "expert", r) for r, chip in zip(far[::2], chips)]
+    other_near = hop(near_grads[0], "expert", 1)
     sum2 = small(join(2, back2 + [up3]))
     home2 = hop(sum2, "fsdp", 2 * inner)
-    sum1 = small(join(1, back1))
+    sum1 = small(join(1, after(back1, sum2)))
     home1 = hop(sum1, "fsdp", inner)
-    back0 = sends(0, back1)
-    for r, other in zip(far[::2], other_gu):
-        chip = small(far_gu[r].astype(F32) + other.astype(F32))
-        arrived_gu.append(hop(chip, "expert", r))
-    other_near = hop(near_grads[0], "expert", 1)
-    sum0 = join(0, back0)
+    back0 = sends(0, sum1)
+    chip = small(near_grads[1].astype(F32) + other_near.astype(F32))
+    (down,) = final_sum([chip] + arrived_down, [(2,)] + [(0,)] * len(arrived_down), True)
+    sum0 = join(0, after(back0, down))
     for got in (home1, home2):
         sum0 = sum0 + got.astype(F32)
-    chip = small(near_grads[1].astype(F32) + other_near.astype(F32))
-    (down,) = final_sum([chip] + arrived_down, [(2,)] + [(0,)] * len(arrived_down), True)
     mixed, d_tokens = small(sum0[:rows]), small(sum0[rows : 2 * rows])
     d_gates = sum0[2 * rows : 2 * rows + 2, :rows].T
     gate, up = final_sum([chip] + arrived_gu, [(0, 1)] * (1 + len(arrived_gu)), False)

time: 215 us -> 211 us (0.981)
  waiting for transfers between devices: 89.8 us -> 79.2 us
  starting transfers between devices: 22.3 us -> 28.8 us
    ppermute x24, waiting for transfers between devices: 89.8 us -> 79.2 us  [hop(): lax.ppermute(value, axis, [(i, i ^ step) for i in range(lax.axis_size(axi...]
    ppermute x24, starting transfers between devices: 22.3 us -> 28.8 us  [hop(): lax.ppermute(value, axis, [(i, i ^ step) for i in range(lax.axis_size(axi...]
    unnamed x44 -> x49, local copies, waits for them, and re-layouts: 7.97 us -> 6.51 us
  transfers between devices with their start and end apart: 24 -> 24, of which waited for: 11 -> 11; matrix products, arithmetic and copies ran while one was open for 5% -> 2% of each run, Pallas kernels for 39% -> 40%
where the time goes in v2:
time: 211 us; the launch traced here: 210 us
  Pallas kernels  86.9 us (41%)
  waiting for transfers between devices  79.2 us (38%)
  starting transfers between devices  28.8 us (14%)
  local copies, waits for them, and re-layouts  8.06 us (4%)
  other arithmetic  6.19 us (3%)
    ppermute x24, waiting for transfers between devices, hop(): lax.ppermute(value, axis, [(i, i ^ step) for i in range(lax.axis_size(axi...  79.2 us
    pallas_call x5, Pallas kernels, block(): pl.pallas_call(functools.partial(block_kernel, tuple(steps), packs, rows,...  60.9 us
    ppermute x24, starting transfers between devices, hop(): lax.ppermute(value, axis, [(i, i ^ step) for i in range(lax.axis_size(axi...  28.8 us
    pallas_call x3, Pallas kernels, grad(): pl.pallas_call(functools.partial(grad_kernel, parts, len(experts)), grid=...  21.7 us
    unnamed x49, local copies, waits for them, and re-layouts  6.51 us
    pallas_call x2, Pallas kernels, final_sum(): pl.pallas_call(functools.partial(final_kernel, places, turned, len(parts)...  4.37 us
  transfers between devices with their start and end apart: 24, of which 11 were waited for; matrix products, arithmetic and copies ran while one was open for 2% of the time, Pallas kernels for 40%

profile of v2, /device:TPU:0, one launch (start us, length us, event | category | flops | bytes accessed | tf_op | source)
XLA Modules:
  0.0 210.0 jit_solution(14226338054429935312)
XLA Ops:
  0.7 0.8 convert_convert_fusion
  1.4 0.7 reduce-precision_convert_fusion
  2.1 1.4 copy.23
  3.6 0.9 fusion.1.refs_0_
  4.6 0.3 copy-done.18
  4.9 0.3 copy-done.19
  5.2 0.2 pad_maximum_fusion.refs_2_.refs_1_
  5.4 0.5 collective-permute-start.4
  5.9 2.6 %collective-permute-start.2 = (bf16[5,768,256]{2,1,0:T(8,128)(2,1)S(1)}, bf16[5,768,256]{2,1,0:T(8,128)(2,1)}, u32[]{:S(2)}, u32[]{:S(2)}) collective-permute-start(bf16[5,768,256]{2,1,0:T(8,128)(2,1)S(1)} %pad_maximum_fusion.refs_2_.refs_1_), channel_id=1, source_target_pairs={{0,16},{8,24},{16,0},{24,8},{1,17},{9,25},{17,1},{25,9},{2,18},{10... | collective-permute-start | bytes 5898248 | tf_op jit(solution)/shard_map/ppermute | solution.py:22
  8.5 0.2 collective-permute-start.5
  8.7 1.5 collective-permute-start.3
  10.2 2.6 %collective-permute-start.1 = (bf16[264,1536]{1,0:T(8,128)(2,1)}, bf16[264,1536]{1,0:T(8,128)(2,1)S(1)}, u32[]{:S(2)}, u32[]{:S(2)}) collective-permute-start(bf16[264,1536]{1,0:T(8,128)(2,1)} %fusion.1.refs_0_), channel_id=1, source_target_pairs={{0,4},{1,5},{2,6},{3,7},{4,0},{5,1},{6,2},{7,3},{8,12},{9,13},{10,... | collective-permute-start | bytes 2433032 | tf_op jit(solution)/shard_map/ppermute | solution.py:22
  12.8 0.7 copy-done.5
  13.5 1.6 collective-permute-start
  15.1 14.2 %collective-permute-done.3.refs_1_ = bf16[264,1536]{1,0:T(8,128)(2,1)} collective-permute-done((bf16[264,1536]{1,0:T(8,128)(2,1)}, bf16[264,1536]{1,0:T(8,128)(2,1)}, u32[]{:S(2)}, u32[]{:S(2)}) %collective-permute-start.3) | collective-permute-done | bytes 811040 | tf_op jit(solution)/shard_map/ppermute | solution.py:22
  29.3 8.9 %block.5 = (bf16[264,1536]{1,0:T(8,128)(2,1)}, bf16[264,1536]{1,0:T(8,128)(2,1)}, bf16[4,3,1024,256]{3,2,1,0:T(8,128)(2,1)}, bf16[1536,1024]{1,0:T(8,128)(2,1)}, bf16[1536,1024]{1,0:T(8,128)(2,1)}) custom-call(s32[1]{0:T(128)} %bitcast.me_ref, bf16[264,1536]{1,0:T(8,128)(2,1)} %fusion.1.refs_0_, bf16[264,1536]{1,0:T(8,128)(2,1)} %collective-permute-done.3.refs_1_, ...), custom_call_target="tpu_custom_call" | custom-call | flops 1000 | bytes 1000 | tf_op jit(solution)/shard_map/block/pallas_call | solution.py:195
  38.2 10.6 %collective-permute-done.1.refs_1_.refs_3_ = bf16[264,1536]{1,0:T(8,128)(2,1)S(1)} collective-permute-done((bf16[264,1536]{1,0:T(8,128)(2,1)}, bf16[264,1536]{1,0:T(8,128)(2,1)S(1)}, u32[]{:S(2)}, u32[]{:S(2)}) %collective-permute-start.1) | collective-permute-done | bytes 811040 | tf_op jit(solution)/shard_map/ppermute | solution.py:22
  48.8 1.0 collective-permute-done.refs_0_.refs_2_
  49.9 2.1 %collective-permute-done.2.refs_4_.refs_5_.refs_6_ = bf16[5,768,256]{2,1,0:T(8,128)(2,1)} collective-permute-done((bf16[5,768,256]{2,1,0:T(8,128)(2,1)S(1)}, bf16[5,768,256]{2,1,0:T(8,128)(2,1)}, u32[]{:S(2)}, u32[]{:S(2)}) %collective-permute-start.2) | collective-permute-done | bytes 1966112 | tf_op jit(solution)/shard_map/ppermute | solution.py:22
  52.0 1.3 pad_maximum_fusion.1
  53.4 1.9 collective-permute-start.10
  55.2 1.6 collective-permute-start.9
  56.8 1.5 collective-permute-start.6
  58.3 8.9 %block.6 = (bf16[264,1536]{1,0:T(8,128)(2,1)}, bf16[264,1536]{1,0:T(8,128)(2,1)}, bf16[4,3,1024,256]{3,2,1,0:T(8,128)(2,1)}, bf16[1536,1024]{1,0:T(8,128)(2,1)}, bf16[1536,1024]{1,0:T(8,128)(2,1)}) custom-call(s32[1]{0:T(128)} %bitcast.me_ref, ...), custom_call_target="tpu_custom_call", output_to_operand_aliasing={{2}: (7, {}), {3}: (8, {}), {4}: (9, {})} | custom-call | flops 1000 | bytes 1000 | tf_op jit(solution)/shard_map/block/pallas_call | solution.py:195
  67.2 0.6 collective-permute-done.6.refs_5_.refs_6_.refs_7_
  67.8 1.7 collective-permute-done.8.refs_7_.refs_8_.refs_9_
  69.6 0.8 copy-done.7
  70.3 14.5 %block.7 = (bf16[264,1536]{1,0:T(8,128)(2,1)}, bf16[264,1536]{1,0:T(8,128)(2,1)}, bf16[264,1536]{1,0:T(8,128)(2,1)}, bf16[264,1536]{1,0:T(8,128)(2,1)}, bf16[4,3,1024,256]{3,2,1,0:T(8,128)(2,1)}) custom-call(s32[1]{0:T(128)} %bitcast.me_ref, bf16[264,1536]{1,0:T(8,128)(2,1)} %fusion.1.refs_0_, ...), custom_call_target="tpu_custom_call", output_to_operand_aliasing={{4}: (13, {})} | custom-call | flops 1000 | bytes 1000 | tf_op jit(solution)/shard_map/block/pallas_call | solution.py:195
  84.9 0.6 collective-permute-start.11
  85.4 6.2 %collective-permute-done.10.refs_0_ = bf16[2,264,1536]{2,1,0:T(8,128)(2,1)S(1)} collective-permute-done((bf16[2,264,1536]{2,1,0:T(8,128)(2,1)S(1)}, bf16[2,264,1536]{2,1,0:T(8,128)(2,1)S(1)}, u32[]{:S(2)}, u32[]{:S(2)}) %collective-permute-start.10) | collective-permute-done | bytes 1622048 | tf_op jit(solution)/shard_map/ppermute | solution.py:22
  91.7 1.2 copy-done.9
  92.8 14.2 %block.8 = (bf16[264,1536]{1,0:T(8,128)(2,1)}, bf16[264,1536]{1,0:T(8,128)(2,1)}, bf16[4,3,1024,256]{3,2,1,0:T(8,128)(2,1)}, bf16[1536,1024]{1,0:T(8,128)(2,1)}, bf16[1536,1024]{1,0:T(8,128)(2,1)}) custom-call(s32[1]{0:T(128)} %bitcast.me_ref, bf16[2,264,1536]{2,1,0:T(8,128)(2,1)} %copy-done.9, ...), custom_call_target="tpu_custom_call", output_to_operand_aliasing={{2}: (10, {}), {3}: (11, {}), {4}: (12, {})} | custom-call | flops 1000 | bytes 1000 | tf_op jit(solution)/shard_map/block/pallas_call | solution.py:195
  107.1 1.9 collective-permute-start.13
  109.0 0.9 copy-done.12
  109.9 14.4 %block.9 = (bf16[264,1536]{1,0:T(8,128)(2,1)}, bf16[264,1536]{1,0:T(8,128)(2,1)}, bf16[4,3,1024,256]{3,2,1,0:T(8,128)(2,1)}, bf16[1536,1024]{1,0:T(8,128)(2,1)}, bf16[1536,1024]{1,0:T(8,128)(2,1)}) custom-call(s32[1]{0:T(128)} %bitcast.me_ref, bf16[264,1536]{1,0:T(8,128)(2,1)} %copy-done.11, ...), custom_call_target="tpu_custom_call", output_to_operand_aliasing={{2}: (11, {}), {3}: (12, {}), {4}: (13, {})} | custom-call | flops 1000 | bytes 1000 | tf_op jit(solution)/shard_map/block/pallas_call | solution.py:195
  124.2 1.6 collective-permute-start.14
  125.8 5.2 %grad.3 = (bf16[1,1536,256]{2,1,0:T(8,128)(2,1)}, bf16[1,1536,256]{2,1,0:T(8,128)(2,1)}) custom-call(s32[1]{0:T(128)} %bitcast.me_ref, bf16[1536,1024]{1,0:T(8,128)(2,1)} %get-tuple-element.119.refs_0_.refs_1_, bf16[4,3,1024,256]{3,2,1,0:T(8,128)(2,1)} %get-tuple-element.117.refs_1_.refs_2_.refs_3_, ...), custom_call_target="tpu_custom_call" | custom-call | flops 1000 | bytes 1000 | tf_op jit(solution)/shard_map/grad/pallas_call | solution.py:237
  131.0 7.0 %grad.4 = (bf16[2,1536,256]{2,1,0:T(8,128)(2,1)}, bf16[2,1536,256]{2,1,0:T(8,128)(2,1)}) custom-call(s32[1]{0:T(128)} %bitcast.me_ref, bf16[1536,1024]{1,0:T(8,128)(2,1)} %get-tuple-element.125.refs_0_, bf16[4,3,1024,256]{3,2,1,0:T(8,128)(2,1)} %get-tuple-element.117.refs_1_.refs_2_.refs_3_, bf16[4,3,1024,256]{3,2,1,0:T(8,128)(2,1)} %get-tuple-element.117.refs_1_.refs_2_.refs_3_), custom_call_target="tpu_custom_call" | custom-call | flops 1000 | bytes 1000 | tf_op jit(solution)/shard_map/grad/pallas_call | solution.py:237
  138.0 0.5 collective-permute-start.18
  138.5 5.7 %collective-permute-done.14 = bf16[264,1536]{1,0:T(8,128)(2,1)S(1)} collective-permute-done((bf16[264,1536]{1,0:T(8,128)(2,1)}, bf16[264,1536]{1,0:T(8,128)(2,1)S(1)}, u32[]{:S(2)}, u32[]{:S(2)}) %collective-permute-start.14) | collective-permute-done | bytes 811040 | tf_op jit(solution)/shard_map/ppermute | solution.py:22
  144.2 0.2 add_convert_fusion.5
  144.4 0.2 add_convert_fusion.4
  144.6 1.8 collective-permute-start.15
  146.4 1.5 collective-permute-start.16
  147.9 1.5 collective-permute-start.17
  149.4 9.4 %grad.5 = (bf16[3,1536,256]{2,1,0:T(8,128)(2,1)}, bf16[3,1536,256]{2,1,0:T(8,128)(2,1)}) custom-call(s32[1]{0:T(128)} %bitcast.me_ref, bf16[1536,1024]{1,0:T(8,128)(2,1)} %get-tuple-element.125.refs_0_, bf16[1536,1024]{1,0:T(8,128)(2,1)} %get-tuple-element.119.refs_0_.refs_1_, bf16[4,3,1024,256]{3,2,1,0:T(8,128)(2,1)} %get-tuple-element.117.refs_1_.refs_2_.refs_3_, ...), custom_call_target="tpu_custom_call" | custom-call | flops 1000 | bytes 1000 | tf_op jit(solution)/shard_map/grad/pallas_call | solution.py:237
  158.9 0.4 add_convert_fusion.1
  159.3 6.6 %collective-permute-done.17.refs_1_ = bf16[1,1536,256]{2,1,0:T(8,128)(2,1)S(1)} collective-permute-done((bf16[1,1536,256]{2,1,0:T(8,128)(2,1)S(1)}, bf16[1,1536,256]{2,1,0:T(8,128)(2,1)S(1)}, u32[]{:S(2)}, u32[]{:S(2)}) %collective-permute-start.17) | collective-permute-done | bytes 786464 | tf_op jit(solution)/shard_map/ppermute | solution.py:22
  165.9 0.1 collective-permute-start.20
  166.0 0.3 add_convert_fusion.3
  166.3 0.8 copy-done.13
  167.1 0.2 add_convert_fusion.2
  167.3 1.0 collective-permute-start.19
  168.3 0.4 collective-permute-start.21
  168.7 2.6 %collective-permute-start.22 = (bf16[264,1536]{1,0:T(8,128)(2,1)S(1)}, bf16[264,1536]{1,0:T(8,128)(2,1)S(1)}, u32[]{:S(2)}, u32[]{:S(2)}) collective-permute-start(bf16[264,1536]{1,0:T(8,128)(2,1)S(1)} %add_convert_fusion.3), channel_id=1, source_target_pairs={{0,4},{1,5},{2,6},{3,7},{4,0},{5,1},{6,2},{7,3},{8,12},{9,13},{10,... | collective-permute-start | bytes 2433032 | tf_op jit(solution)/shard_map/ppermute | solution.py:22
  171.3 1.5 collective-permute-start.23
  172.8 0.5 add_convert_fusion.refs_0_
  173.4 2.1 %final.2 = f32[1,256,1536]{2,1,0:T(8,128)} custom-call(bf16[3,1536,256]{2,1,0:T(8,128)(2,1)S(1)} %add_convert_fusion.refs_0_, bf16[1,1536,256]{2,1,0:T(8,128)(2,1)S(1)} %collective-permute-done.17.refs_1_), custom_call_target="tpu_custom_call" | custom-call | flops 1000 | bytes 1000 | tf_op jit(solution)/shard_map/final/pallas_call | solution.py:267
  175.5 12.3 %collective-permute-done.19 = bf16[264,1536]{1,0:T(8,128)(2,1)S(1)} collective-permute-done((bf16[264,1536]{1,0:T(8,128)(2,1)S(1)}, bf16[264,1536]{1,0:T(8,128)(2,1)S(1)}, u32[]{:S(2)}, u32[]{:S(2)}) %collective-permute-start.19) | collective-permute-done | bytes 811040 | tf_op jit(solution)/shard_map/ppermute | solution.py:22
  187.8 18.0 %collective-permute-done.21 = bf16[264,1536]{1,0:T(8,128)(2,1)S(1)} collective-permute-done((bf16[264,1536]{1,0:T(8,128)(2,1)S(1)}, bf16[264,1536]{1,0:T(8,128)(2,1)S(1)}, u32[]{:S(2)}, u32[]{:S(2)}) %collective-permute-start.21) | collective-permute-done | bytes 811040 | tf_op jit(solution)/shard_map/ppermute | solution.py:22
  205.9 0.4 fusion.3
  206.3 0.6 slice_bitcast_fusion.2
  206.9 0.9 fusion.4
  207.8 2.2 %final.3 = (f32[1,1536,256]{2,1,0:T(8,128)}, f32[1,1536,256]{2,1,0:T(8,128)}) custom-call(bf16[3,1536,256]{2,1,0:T(8,128)(2,1)S(1)} %add_convert_fusion.refs_0_, bf16[2,1536,256]{2,1,0:T(8,128)(2,1)S(1)} %collective-permute-done.23.refs_1_), custom_call_target="tpu_custom_call" | custom-call | flops 1000 | bytes 1000 | tf_op jit(solution)/shard_map/final/pallas_call | solution.py:267
  (59 shorter events, 0.3 us)
Async XLA Ops:
  0.6 2.9 %copy-start.20 = (bf16[128,1536]{1,0:T(8,128)(2,1)S(1)}, bf16[128,1536]{1,0:T(8,128)(2,1)}, u32[]{:S(2)}) copy-start(bf16[128,1536]{1,0:T(8,128)(2,1)} %param.10) | copy-start | bytes 1179652
  0.6 2.9 %copy-start.21 = (bf16[128,1536]{1,0:T(8,128)(2,1)S(1)}, bf16[128,1536]{1,0:T(8,128)(2,1)}, u32[]{:S(2)}) copy-start(bf16[128,1536]{1,0:T(8,128)(2,1)} %param.7) | copy-start | bytes 1179652
  3.5 1.4 copy-start.18
  3.5 1.7 copy-start.19
  4.6 3.9 %copy-start.2 = (bf16[1,768,256]{2,1,0:T(8,128)(2,1)}, bf16[1,768,256]{2,1,0:T(8,128)(2,1)S(1)}, u32[]{:S(2)}) copy-start(bf16[1,768,256]{2,1,0:T(8,128)(2,1)S(1)} %get-tuple-element.83.refs_3_.refs_2_) | copy-start | bytes 1179652
  5.4 23.9 %copy-start = (bf16[5,768,256]{2,1,0:T(8,128)(2,1)}, bf16[5,768,256]{2,1,0:T(8,128)(2,1)S(1)}, u32[]{:S(2)}) copy-start(bf16[5,768,256]{2,1,0:T(8,128)(2,1)S(1)} %pad_maximum_fusion.refs_2_.refs_1_) | copy-start | bytes 5898244
  5.4 23.9 %collective-permute-start.4 = (bf16[5,768,256]{2,1,0:T(8,128)(2,1)S(1)}, bf16[5,768,256]{2,1,0:T(8,128)(2,1)}, u32[]{:S(2)}, u32[]{:S(2)}) collective-permute-start(bf16[5,768,256]{2,1,0:T(8,128)(2,1)S(1)} %pad_maximum_fusion.refs_2_.refs_1_), channel_id=1, source_target_pairs={{0,8},{8,0},{16,24},{24,16},{1,9},{9,1},{17,25},{25,17},{2,10},{10... | collective-permute-start | bytes 5898248 | tf_op jit(solution)/shard_map/ppermute | solution.py:22
  5.9 46.1 %collective-permute-start.2 = (bf16[5,768,256]{2,1,0:T(8,128)(2,1)S(1)}, bf16[5,768,256]{2,1,0:T(8,128)(2,1)}, u32[]{:S(2)}, u32[]{:S(2)}) collective-permute-start(bf16[5,768,256]{2,1,0:T(8,128)(2,1)S(1)} %pad_maximum_fusion.refs_2_.refs_1_), channel_id=1, source_target_pairs={{0,16},{8,24},{16,0},{24,8},{1,17},{9,25},{17,1},{25,9},{2,18},{10... | collective-permute-start | bytes 5898248 | tf_op jit(solution)/shard_map/ppermute | solution.py:22
  8.5 4.3 %collective-permute-start.5 = (bf16[1,768,256]{2,1,0:T(8,128)(2,1)S(1)}, bf16[1,768,256]{2,1,0:T(8,128)(2,1)S(1)}, u32[]{:S(2)}, u32[]{:S(2)}) collective-permute-start(bf16[1,768,256]{2,1,0:T(8,128)(2,1)S(1)} %get-tuple-element.83.refs_3_.refs_2_), channel_id=1, source_target_pairs={{0,8},{8,0},{16,24},{24,16},{1,9},{9,1},{17,25},{25,17},{2,10},{10... | collective-permute-start | bytes 1179656 | tf_op jit(solution)/shard_map/ppermute | solution.py:22
  8.7 20.6 %collective-permute-start.3 = (bf16[264,1536]{1,0:T(8,128)(2,1)}, bf16[264,1536]{1,0:T(8,128)(2,1)}, u32[]{:S(2)}, u32[]{:S(2)}) collective-permute-start(bf16[264,1536]{1,0:T(8,128)(2,1)} %fusion.1.refs_0_), channel_id=1, source_target_pairs={{0,1},{1,0},{2,3},{3,2},{4,5},{5,4},{6,7},{7,6},{8,9},{9,8},{10,11... | collective-permute-start | bytes 2433032 | tf_op jit(solution)/shard_map/ppermute | solution.py:22
  10.2 38.7 %collective-permute-start.1 = (bf16[264,1536]{1,0:T(8,128)(2,1)}, bf16[264,1536]{1,0:T(8,128)(2,1)S(1)}, u32[]{:S(2)}, u32[]{:S(2)}) collective-permute-start(bf16[264,1536]{1,0:T(8,128)(2,1)} %fusion.1.refs_0_), channel_id=1, source_target_pairs={{0,4},{1,5},{2,6},{3,7},{4,0},{5,1},{6,2},{7,3},{8,12},{9,13},{10,... | collective-permute-start | bytes 2433032 | tf_op jit(solution)/shard_map/ppermute | solution.py:22
  12.8 0.7 copy-start.5
  13.5 36.3 %collective-permute-start = (bf16[264,1536]{1,0:T(8,128)(2,1)}, bf16[264,1536]{1,0:T(8,128)(2,1)}, u32[]{:S(2)}, u32[]{:S(2)}) collective-permute-start(bf16[264,1536]{1,0:T(8,128)(2,1)} %fusion.1.refs_0_), channel_id=1, source_target_pairs={{0,2},{1,3},{2,0},{3,1},{4,6},{5,7},{6,4},{7,5},{8,10},{9,11},{10,... | collective-permute-start | bytes 2433032 | tf_op jit(solution)/shard_map/ppermute | solution.py:22
  48.8 6.4 %copy-start.4 = (bf16[264,1536]{1,0:T(8,128)(2,1)}, bf16[264,1536]{1,0:T(8,128)(2,1)S(1)}, u32[]{:S(2)}) copy-start(bf16[264,1536]{1,0:T(8,128)(2,1)S(1)} %collective-permute-done.1.refs_1_.refs_3_) | copy-start | bytes 2433028
  52.0 15.8 %collective-permute-start.7 = (bf16[5,768,256]{2,1,0:T(8,128)(2,1)}, bf16[5,768,256]{2,1,0:T(8,128)(2,1)S(1)}, u32[]{:S(2)}, u32[]{:S(2)}) collective-permute-start(bf16[5,768,256]{2,1,0:T(8,128)(2,1)} %collective-permute-done.2.refs_4_.refs_5_.refs_6_), channel_id=1, source_target_pairs={{0,8},{8,0},{16,24},{24,16},{1,9},{9,1},{17,25},{25,17},{2,10},{10... | collective-permute-start | bytes 5898248 | tf_op jit(solution)/shard_map/ppermute | solution.py:22
  52.0 4.8 %copy-start.3 = (bf16[1,768,256]{2,1,0:T(8,128)(2,1)S(1)}, bf16[1,768,256]{2,1,0:T(8,128)(2,1)}, u32[]{:S(2)}) copy-start(bf16[1,768,256]{2,1,0:T(8,128)(2,1)} %copy-done.2) | copy-start | bytes 1179652
  53.4 38.3 %collective-permute-start.10 = (bf16[2,264,1536]{2,1,0:T(8,128)(2,1)S(1)}, bf16[2,264,1536]{2,1,0:T(8,128)(2,1)S(1)}, u32[]{:S(2)}, u32[]{:S(2)}) collective-permute-start(bf16[2,264,1536]{2,1,0:T(8,128)(2,1)S(1)} %pad_maximum_fusion.1), channel_id=1, source_target_pairs={{0,1},{1,0},{2,3},{3,2},{4,5},{5,4},{6,7},{7,6},{8,9},{9,8},{10,11... | collective-permute-start | bytes 4866056 | tf_op jit(solution)/shard_map/ppermute | solution.py:22
  55.2 29.6 %collective-permute-start.9 = (bf16[264,1536]{1,0:T(8,128)(2,1)S(1)}, bf16[264,1536]{1,0:T(8,128)(2,1)S(1)}, u32[]{:S(2)}, u32[]{:S(2)}) collective-permute-start(bf16[264,1536]{1,0:T(8,128)(2,1)S(1)} %collective-permute-done.1.refs_1_.refs_3_), channel_id=1, source_target_pairs={{0,2},{1,3},{2,0},{3,1},{4,6},{5,7},{6,4},{7,5},{8,10},{9,11},{10,... | collective-permute-start | bytes 2433032 | tf_op jit(solution)/shard_map/ppermute | solution.py:22
  56.8 11.0 %collective-permute-start.6 = (bf16[1,768,256]{2,1,0:T(8,128)(2,1)S(1)}, bf16[1,768,256]{2,1,0:T(8,128)(2,1)S(1)}, u32[]{:S(2)}, u32[]{:S(2)}) collective-permute-start(bf16[1,768,256]{2,1,0:T(8,128)(2,1)S(1)} %copy-done.3), channel_id=1, source_target_pairs={{0,16},{8,24},{16,0},{24,8},{1,17},{9,25},{17,1},{25,9},{2,18},{10... | collective-permute-start | bytes 1179656 | tf_op jit(solution)/shard_map/ppermute | solution.py:22
  67.8 1.8 copy-start.6
  67.8 1.8 copy-start.1
  67.8 1.8 collective-permute-start.8
  69.6 0.8 copy-start.7
  84.8 22.3 %copy-start.11 = (bf16[264,1536]{1,0:T(8,128)(2,1)}, bf16[264,1536]{1,0:T(8,128)(2,1)S(1)}, u32[]{:S(2)}) copy-start(bf16[264,1536]{1,0:T(8,128)(2,1)S(1)} %collective-permute-done.9.refs_0_) | copy-start | bytes 2433028
  84.9 24.1 %collective-permute-start.11 = (bf16[264,1536]{1,0:T(8,128)(2,1)S(1)}, bf16[264,1536]{1,0:T(8,128)(2,1)S(1)}, u32[]{:S(2)}, u32[]{:S(2)}) collective-permute-start(bf16[264,1536]{1,0:T(8,128)(2,1)S(1)} %collective-permute-done.9.refs_0_), channel_id=1, source_target_pairs={{0,1},{1,0},{2,3},{3,2},{4,5},{5,4},{6,7},{7,6},{8,9},{9,8},{10,11... | collective-permute-start | bytes 2433032 | tf_op jit(solution)/shard_map/ppermute | solution.py:22
  91.7 1.2 copy-start.9
  107.1 31.4 %collective-permute-start.13 = (bf16[264,1536]{1,0:T(8,128)(2,1)}, bf16[264,1536]{1,0:T(8,128)(2,1)S(1)}, u32[]{:S(2)}, u32[]{:S(2)}) collective-permute-start(bf16[264,1536]{1,0:T(8,128)(2,1)} %get-tuple-element.121), channel_id=1, source_target_pairs={{0,1},{1,0},{2,3},{3,2},{4,5},{5,4},{6,7},{7,6},{8,9},{9,8},{10,11... | collective-permute-start | bytes 2433032 | tf_op jit(solution)/shard_map/ppermute | solution.py:22
  109.0 0.9 copy-start.12
  124.2 20.0 %collective-permute-start.14 = (bf16[264,1536]{1,0:T(8,128)(2,1)}, bf16[264,1536]{1,0:T(8,128)(2,1)S(1)}, u32[]{:S(2)}, u32[]{:S(2)}) collective-permute-start(bf16[264,1536]{1,0:T(8,128)(2,1)} %get-tuple-element.122), channel_id=1, source_target_pairs={{0,1},{1,0},{2,3},{3,2},{4,5},{5,4},{6,7},{7,6},{8,9},{9,8},{10,11... | collective-permute-start | bytes 2433032 | tf_op jit(solution)/shard_map/ppermute | solution.py:22
  130.9 7.5 %collective-permute-start.12 = (bf16[1,1536,256]{2,1,0:T(8,128)(2,1)}, bf16[1,1536,256]{2,1,0:T(8,128)(2,1)S(1)}, u32[]{:S(2)}, u32[]{:S(2)}) collective-permute-start(bf16[1,1536,256]{2,1,0:T(8,128)(2,1)} %get-tuple-element.120), channel_id=1, source_target_pairs={{0,8},{8,0},{16,24},{24,16},{1,9},{9,1},{17,25},{25,17},{2,10},{10... | collective-permute-start | bytes 2359304 | tf_op jit(solution)/shard_map/ppermute | solution.py:22
  130.9 13.2 %copy-start.17 = (bf16[1,1536,256]{2,1,0:T(8,128)(2,1)S(1)}, bf16[1,1536,256]{2,1,0:T(8,128)(2,1)}, u32[]{:S(2)}) copy-start(bf16[1,1536,256]{2,1,0:T(8,128)(2,1)} %get-tuple-element.123) | copy-start | bytes 2359300
  138.0 6.4 %copy-start.15 = (bf16[264,1536]{1,0:T(8,128)(2,1)S(1)}, bf16[264,1536]{1,0:T(8,128)(2,1)}, u32[]{:S(2)}) copy-start(bf16[264,1536]{1,0:T(8,128)(2,1)} %get-tuple-element.116) | copy-start | bytes 2433028
  138.0 20.9 %collective-permute-start.18 = (bf16[2,1536,256]{2,1,0:T(8,128)(2,1)}, bf16[2,1536,256]{2,1,0:T(8,128)(2,1)S(1)}, u32[]{:S(2)}, u32[]{:S(2)}) collective-permute-start(bf16[2,1536,256]{2,1,0:T(8,128)(2,1)} %get-tuple-element.127), channel_id=1, source_target_pairs={{0,8},{8,0},{16,24},{24,16},{1,9},{9,1},{17,25},{25,17},{2,10},{10... | collective-permute-start | bytes 4718600 | tf_op jit(solution)/shard_map/ppermute | solution.py:22
  144.6 14.3 %copy-start.10 = (bf16[2,1536,256]{2,1,0:T(8,128)(2,1)S(1)}, bf16[2,1536,256]{2,1,0:T(8,128)(2,1)}, u32[]{:S(2)}) copy-start(bf16[2,1536,256]{2,1,0:T(8,128)(2,1)} %get-tuple-element.126) | copy-start | bytes 4718596
  144.6 21.2 %collective-permute-start.15 = (bf16[264,1536]{1,0:T(8,128)(2,1)S(1)}, bf16[264,1536]{1,0:T(8,128)(2,1)S(1)}, u32[]{:S(2)}, u32[]{:S(2)}) collective-permute-start(bf16[264,1536]{1,0:T(8,128)(2,1)S(1)} %add_convert_fusion.4), channel_id=1, source_target_pairs={{0,2},{1,3},{2,0},{3,1},{4,6},{5,7},{6,4},{7,5},{8,10},{9,11},{10,... | collective-permute-start | bytes 2433032 | tf_op jit(solution)/shard_map/ppermute | solution.py:22
  146.4 19.4 %collective-permute-start.16 = (bf16[264,1536]{1,0:T(8,128)(2,1)}, bf16[264,1536]{1,0:T(8,128)(2,1)S(1)}, u32[]{:S(2)}, u32[]{:S(2)}) collective-permute-start(bf16[264,1536]{1,0:T(8,128)(2,1)} %get-tuple-element.133), channel_id=1, source_target_pairs={{0,1},{1,0},{2,3},{3,2},{4,5},{5,4},{6,7},{7,6},{8,9},{9,8},{10,11... | collective-permute-start | bytes 2433032 | tf_op jit(solution)/shard_map/ppermute | solution.py:22
  147.9 17.9 %collective-permute-start.17 = (bf16[1,1536,256]{2,1,0:T(8,128)(2,1)S(1)}, bf16[1,1536,256]{2,1,0:T(8,128)(2,1)S(1)}, u32[]{:S(2)}, u32[]{:S(2)}) collective-permute-start(bf16[1,1536,256]{2,1,0:T(8,128)(2,1)S(1)} %add_convert_fusion.5), channel_id=1, source_target_pairs={{0,16},{8,24},{16,0},{24,8},{1,17},{9,25},{17,1},{25,9},{2,18},{10... | collective-permute-start | bytes 2359304 | tf_op jit(solution)/shard_map/ppermute | solution.py:22
  158.9 7.0 %copy-start.22 = (bf16[3,1536,256]{2,1,0:T(8,128)(2,1)S(1)}, bf16[3,1536,256]{2,1,0:T(8,128)(2,1)}, u32[]{:S(2)}) copy-start(bf16[3,1536,256]{2,1,0:T(8,128)(2,1)} %get-tuple-element.144) | copy-start | bytes 7077892
  158.9 7.0 %copy-start.14 = (bf16[264,1536]{1,0:T(8,128)(2,1)S(1)}, bf16[264,1536]{1,0:T(8,128)(2,1)}, u32[]{:S(2)}) copy-start(bf16[264,1536]{1,0:T(8,128)(2,1)} %get-tuple-element.139) | copy-start | bytes 2433028
  165.9 7.0 %collective-permute-start.20 = (bf16[3,1536,256]{2,1,0:T(8,128)(2,1)S(1)}, bf16[3,1536,256]{2,1,0:T(8,128)(2,1)S(1)}, u32[]{:S(2)}, u32[]{:S(2)}) collective-permute-start(bf16[3,1536,256]{2,1,0:T(8,128)(2,1)S(1)} %copy-done.22), channel_id=1, source_target_pairs={{0,8},{8,0},{16,24},{24,16},{1,9},{9,1},{17,25},{25,17},{2,10},{10... | collective-permute-start | bytes 7077896 | tf_op jit(solution)/shard_map/ppermute | solution.py:22
  166.0 1.1 copy-start.13
  166.0 1.4 copy-start.23
  166.3 6.6 %copy-start.8 = (bf16[3,1536,256]{2,1,0:T(8,128)(2,1)S(1)}, bf16[3,1536,256]{2,1,0:T(8,128)(2,1)}, u32[]{:S(2)}) copy-start(bf16[3,1536,256]{2,1,0:T(8,128)(2,1)} %get-tuple-element.143) | copy-start | bytes 7077892
  167.3 20.5 %collective-permute-start.19 = (bf16[264,1536]{1,0:T(8,128)(2,1)S(1)}, bf16[264,1536]{1,0:T(8,128)(2,1)S(1)}, u32[]{:S(2)}, u32[]{:S(2)}) collective-permute-start(bf16[264,1536]{1,0:T(8,128)(2,1)S(1)} %copy-done.23), channel_id=1, source_target_pairs={{0,1},{1,0},{2,3},{3,2},{4,5},{5,4},{6,7},{7,6},{8,9},{9,8},{10,11... | collective-permute-start | bytes 2433032 | tf_op jit(solution)/shard_map/ppermute | solution.py:22
  168.3 37.6 %collective-permute-start.21 = (bf16[264,1536]{1,0:T(8,128)(2,1)S(1)}, bf16[264,1536]{1,0:T(8,128)(2,1)S(1)}, u32[]{:S(2)}, u32[]{:S(2)}) collective-permute-start(bf16[264,1536]{1,0:T(8,128)(2,1)S(1)} %add_convert_fusion.2), channel_id=1, source_target_pairs={{0,2},{1,3},{2,0},{3,1},{4,6},{5,7},{6,4},{7,5},{8,10},{9,11},{10,... | collective-permute-start | bytes 2433032 | tf_op jit(solution)/shard_map/ppermute | solution.py:22
  168.7 37.1 %collective-permute-start.22 = (bf16[264,1536]{1,0:T(8,128)(2,1)S(1)}, bf16[264,1536]{1,0:T(8,128)(2,1)S(1)}, u32[]{:S(2)}, u32[]{:S(2)}) collective-permute-start(bf16[264,1536]{1,0:T(8,128)(2,1)S(1)} %add_convert_fusion.3), channel_id=1, source_target_pairs={{0,4},{1,5},{2,6},{3,7},{4,0},{5,1},{6,2},{7,3},{8,12},{9,13},{10,... | collective-permute-start | bytes 2433032 | tf_op jit(solution)/shard_map/ppermute | solution.py:22
  171.3 36.5 %collective-permute-start.23 = (bf16[2,1536,256]{2,1,0:T(8,128)(2,1)S(1)}, bf16[2,1536,256]{2,1,0:T(8,128)(2,1)S(1)}, u32[]{:S(2)}, u32[]{:S(2)}) collective-permute-start(bf16[2,1536,256]{2,1,0:T(8,128)(2,1)S(1)} %add_convert_fusion.1), channel_id=1, source_target_pairs={{0,16},{8,24},{16,0},{24,8},{1,17},{9,25},{17,1},{25,9},{2,18},{10... | collective-permute-start | bytes 4718600 | tf_op jit(solution)/shard_map/ppermute | solution.py:22
  173.4 32.5 %copy-start.16 = (bf16[264,1536]{1,0:T(8,128)(2,1)S(1)}, bf16[264,1536]{1,0:T(8,128)(2,1)}, u32[]{:S(2)}) copy-start(bf16[264,1536]{1,0:T(8,128)(2,1)} %get-tuple-element.101) | copy-start | bytes 2433028

commit v3 on v2

--- a/solution.py
+++ b/solution.py
@@ -339,9 +339,8 @@
     first, second, gus, shared = lax.optimization_barrier((first, second, gus, shared))
 
     pays[1, 0], pays[2, 0] = first, second
-    pair = beside(jnp.stack([first, second]))
-    for j, p in enumerate(pair):
-        pays[1, j + 1], pays[2, j + 1] = (p, 0), (p, 1)
+    for j, p in enumerate(beside(first)):
+        pays[1, j + 1] = p
     third = hop(second, "fsdp", inner)
     for r, gu in zip(far[::2], gus):
         weights[r][0] = gu
@@ -352,24 +351,27 @@
         compute(near, [(1, 0), (2, 0)], me, True)
     downs = [weights[r][1] for r in far[::2]]
     gus = [weights[r + 1][0] for r in far[::2]]
-    downs, gus, shared = lax.optimization_barrier((downs, gus, shared))
+    firsts = [pays[1, j] for j in range(1, inner)]
+    third, firsts, downs, gus, shared = lax.optimization_barrier((third, firsts, downs, gus, shared))
     for r, gu, down in zip(far[::2], gus, downs):
         weights[r][1] = down
         weights[r + 1] = [gu, hop(down, "expert", 1)]
 
-    if split:
-        compute(far, row_of(0) + [(1, 0), (2, 0)], me, False)
-    else:
-        compute(far, row_of(0), me, False)
-    third, shared = lax.optimization_barrier((third, shared))
-    for j, p in enumerate([third] + beside(third)):
+    for j in range(1, inner):
+        pays[1, j] = firsts[j - 1]
+    thirds = [third] + beside(third)
+    compute(far, row_of(0) + [(1, 0), (2, 0)] if split else row_of(0), me, False)
+    thirds, shared, second = lax.optimization_barrier((thirds, shared, second))
+    for j, p in enumerate(thirds):
         pays[3, j] = p
+    for j, p in enumerate(beside(second)):
+        pays[2, j + 1] = p
+    compute(near + far, row_of(3), me, True)
     if split:
         compute(near + far, [(1, 1), (2, 1)], me, True)
     else:
         for k in (1, 2):
             compute(near + far, row_of(k), me, True)
-    compute(near + far, row_of(3), me, True)
 
     small = lambda v: v.astype(BF16)
 

time: 211 us -> 211 us (level)
  waiting for transfers between devices: 79.2 us -> 83.5 us
  other arithmetic: 6.19 us -> 3.98 us
    ppermute x24 -> x25, waiting for transfers between devices: 79.2 us -> 83.5 us  [hop(): lax.ppermute(value, axis, [(i, i ^ step) for i in range(lax.axis_size(axi...]
    ppermute x24 -> x25, starting transfers between devices: 28.8 us -> 28.1 us  [hop(): lax.ppermute(value, axis, [(i, i ^ step) for i in range(lax.axis_size(axi...]
    unnamed x49 -> x51, local copies, waits for them, and re-layouts: 6.51 us -> 5.84 us
  transfers between devices with their start and end apart: 24 -> 25, of which waited for: 11 -> 15; matrix products, arithmetic and copies ran while one was open for 2% -> 2% of each run, Pallas kernels for 40% -> 40%
where the time goes in v3:
time: 211 us
  Pallas kernels  87 us (41%)
  waiting for transfers between devices  83.5 us (40%)
  starting transfers between devices  28.1 us (13%)
  local copies, waits for them, and re-layouts  7.39 us (4%)
  other arithmetic  3.98 us (2%)
    ppermute x25, waiting for transfers between devices, hop(): lax.ppermute(value, axis, [(i, i ^ step) for i in range(lax.axis_size(axi...  83.5 us
    pallas_call x5, Pallas kernels, block(): pl.pallas_call(functools.partial(block_kernel, tuple(steps), packs, rows,...  60.9 us
    ppermute x25, starting transfers between devices, hop(): lax.ppermute(value, axis, [(i, i ^ step) for i in range(lax.axis_size(axi...  28.1 us
    pallas_call x3, Pallas kernels, grad(): pl.pallas_call(functools.partial(grad_kernel, parts, len(experts)), grid=...  21.7 us
    unnamed x51, local copies, waits for them, and re-layouts  5.84 us
    pallas_call x2, Pallas kernels, final_sum(): pl.pallas_call(functools.partial(final_kernel, places, turned, len(parts)...  4.37 us
  transfers between devices with their start and end apart: 25, of which 15 were waited for; matrix products, arithmetic and copies ran while one was open for 2% of the time, Pallas kernels for 40%

profile of v3, /device:TPU:0, one launch (start us, length us, event | category | flops | bytes accessed | tf_op | source)
XLA Modules:
  0.0 210.8 jit_solution(15307059699217041625)
XLA Ops:
  0.7 0.8 convert_convert_fusion
  1.4 0.7 reduce-precision_convert_fusion
  2.1 1.4 copy.23
  3.7 1.2 copy-done.19
  4.9 0.4 copy-done.20
  5.3 0.2 pad_maximum_fusion.refs_2_
  5.5 0.5 collective-permute-start.4
  6.1 2.6 %collective-permute-start.2 = (bf16[5,768,256]{2,1,0:T(8,128)(2,1)S(1)}, bf16[5,768,256]{2,1,0:T(8,128)(2,1)}, u32[]{:S(2)}, u32[]{:S(2)}) collective-permute-start(bf16[5,768,256]{2,1,0:T(8,128)(2,1)S(1)} %pad_maximum_fusion.refs_2_), channel_id=1, source_target_pairs={{0,16},{8,24},{16,0},{24,8},{1,17},{9,25},{17,1},{25,9},{2,18},{10... | collective-permute-start | bytes 5898248 | tf_op jit(solution)/shard_map/ppermute | solution.py:22
  8.8 1.5 collective-permute-start.3
  10.3 2.6 %collective-permute-start.1 = (bf16[264,1536]{1,0:T(8,128)(2,1)S(1)}, bf16[264,1536]{1,0:T(8,128)(2,1)}, u32[]{:S(2)}, u32[]{:S(2)}) collective-permute-start(bf16[264,1536]{1,0:T(8,128)(2,1)S(1)} %fusion.1.refs_0_), channel_id=1, source_target_pairs={{0,4},{1,5},{2,6},{3,7},{4,0},{5,1},{6,2},{7,3},{8,12},{9,13},{10,... | collective-permute-start | bytes 2433032 | tf_op jit(solution)/shard_map/ppermute | solution.py:22
  12.9 1.6 collective-permute-start
  14.6 14.7 %collective-permute-done.3.refs_1_ = bf16[264,1536]{1,0:T(8,128)(2,1)} collective-permute-done((bf16[264,1536]{1,0:T(8,128)(2,1)S(1)}, bf16[264,1536]{1,0:T(8,128)(2,1)}, u32[]{:S(2)}, u32[]{:S(2)}) %collective-permute-start.3) | collective-permute-done | bytes 811040 | tf_op jit(solution)/shard_map/ppermute | solution.py:22
  29.2 8.9 %block.5 = (bf16[264,1536]{1,0:T(8,128)(2,1)}, bf16[264,1536]{1,0:T(8,128)(2,1)}, bf16[4,3,1024,256]{3,2,1,0:T(8,128)(2,1)}, bf16[1536,1024]{1,0:T(8,128)(2,1)}, bf16[1536,1024]{1,0:T(8,128)(2,1)}) custom-call(s32[1]{0:T(128)} %bitcast.me_ref, bf16[264,1536]{1,0:T(8,128)(2,1)} %copy-done.4, bf16[264,1536]{1,0:T(8,128)(2,1)} %collective-permute-done.3.refs_1_, ...), custom_call_target="tpu_custom_call" | custom-call | flops 1000 | bytes 1000 | tf_op jit(solution)/shard_map/block/pallas_call | solution.py:195
  38.2 10.7 %collective-permute-done.1.refs_1_.refs_3_ = bf16[264,1536]{1,0:T(8,128)(2,1)} collective-permute-done((bf16[264,1536]{1,0:T(8,128)(2,1)S(1)}, bf16[264,1536]{1,0:T(8,128)(2,1)}, u32[]{:S(2)}, u32[]{:S(2)}) %collective-permute-start.1) | collective-permute-done | bytes 811040 | tf_op jit(solution)/shard_map/ppermute | solution.py:22
  48.9 0.3 collective-permute-done.refs_0_.refs_2_
  49.1 3.0 %collective-permute-done.2.refs_4_.refs_6_ = bf16[5,768,256]{2,1,0:T(8,128)(2,1)} collective-permute-done((bf16[5,768,256]{2,1,0:T(8,128)(2,1)S(1)}, bf16[5,768,256]{2,1,0:T(8,128)(2,1)}, u32[]{:S(2)}, u32[]{:S(2)}) %collective-permute-start.2) | collective-permute-done | bytes 1966112 | tf_op jit(solution)/shard_map/ppermute | solution.py:22
  52.2 1.8 collective-permute-start.7
  53.9 1.6 collective-permute-start.6
  55.5 1.5 collective-permute-start.8
  57.0 8.9 %block.6 = (bf16[264,1536]{1,0:T(8,128)(2,1)}, bf16[264,1536]{1,0:T(8,128)(2,1)}, bf16[4,3,1024,256]{3,2,1,0:T(8,128)(2,1)}, bf16[1536,1024]{1,0:T(8,128)(2,1)}, bf16[1536,1024]{1,0:T(8,128)(2,1)}) custom-call(s32[1]{0:T(128)} %bitcast.me_ref, ...), custom_call_target="tpu_custom_call", output_to_operand_aliasing={{2}: (7, {}), {3}: (8, {}), {4}: (9, {})} | custom-call | flops 1000 | bytes 1000 | tf_op jit(solution)/shard_map/block/pallas_call | solution.py:195
  65.9 0.5 collective-permute-done.8.refs_5_.refs_7_
  66.5 6.4 %collective-permute-done.7.refs_0_ = bf16[264,1536]{1,0:T(8,128)(2,1)S(1)} collective-permute-done((bf16[264,1536]{1,0:T(8,128)(2,1)}, bf16[264,1536]{1,0:T(8,128)(2,1)S(1)}, u32[]{:S(2)}, u32[]{:S(2)}) %collective-permute-start.7) | collective-permute-done | bytes 811040 | tf_op jit(solution)/shard_map/ppermute | solution.py:22
  72.9 1.5 collective-permute-done.6.refs_0_
  74.4 0.4 collective-permute-start.11
  74.8 1.7 collective-permute-done.10.refs_7_.refs_9_
  76.5 0.7 copy-done.7
  77.2 14.5 %block.7 = (bf16[264,1536]{1,0:T(8,128)(2,1)}, bf16[264,1536]{1,0:T(8,128)(2,1)}, bf16[264,1536]{1,0:T(8,128)(2,1)}, bf16[264,1536]{1,0:T(8,128)(2,1)}, bf16[4,3,1024,256]{3,2,1,0:T(8,128)(2,1)}) custom-call(s32[1]{0:T(128)} %bitcast.me_ref, bf16[264,1536]{1,0:T(8,128)(2,1)} %copy-done.4, ...), custom_call_target="tpu_custom_call", output_to_operand_aliasing={{4}: (13, {})} | custom-call | flops 1000 | bytes 1000 | tf_op jit(solution)/shard_map/block/pallas_call | solution.py:195
  91.8 2.0 collective-permute-done.11.refs_1_
  93.8 0.6 collective-permute-start.12
  94.4 0.3 copy-done.12
  94.7 14.2 %block.8 = (bf16[264,1536]{1,0:T(8,128)(2,1)}, bf16[264,1536]{1,0:T(8,128)(2,1)}, bf16[4,3,1024,256]{3,2,1,0:T(8,128)(2,1)}, bf16[1536,1024]{1,0:T(8,128)(2,1)}, bf16[1536,1024]{1,0:T(8,128)(2,1)}) custom-call(s32[1]{0:T(128)} %bitcast.me_ref, bf16[264,1536]{1,0:T(8,128)(2,1)} %copy-done.11, ...), custom_call_target="tpu_custom_call", output_to_operand_aliasing={{2}: (11, {}), {3}: (12, {}), {4}: (13, {})} | custom-call | flops 1000 | bytes 1000 | tf_op jit(solution)/shard_map/block/pallas_call | solution.py:195
  108.8 1.2 collective-permute-start.15
  110.1 4.4 %collective-permute-done.12.refs_1_ = bf16[264,1536]{1,0:T(8,128)(2,1)S(1)} collective-permute-done((bf16[264,1536]{1,0:T(8,128)(2,1)}, bf16[264,1536]{1,0:T(8,128)(2,1)S(1)}, u32[]{:S(2)}, u32[]{:S(2)}) %collective-permute-start.12) | collective-permute-done | bytes 811040 | tf_op jit(solution)/shard_map/ppermute | solution.py:22
  114.4 0.9 copy-done.13
  115.3 14.4 %block.9 = (bf16[264,1536]{1,0:T(8,128)(2,1)}, bf16[264,1536]{1,0:T(8,128)(2,1)}, bf16[4,3,1024,256]{3,2,1,0:T(8,128)(2,1)}, bf16[1536,1024]{1,0:T(8,128)(2,1)}, bf16[1536,1024]{1,0:T(8,128)(2,1)}) custom-call(s32[1]{0:T(128)} %bitcast.me_ref, bf16[264,1536]{1,0:T(8,128)(2,1)} %copy-done.10, ...), custom_call_target="tpu_custom_call", output_to_operand_aliasing={{2}: (11, {}), {3}: (12, {}), {4}: (13, {})} | custom-call | flops 1000 | bytes 1000 | tf_op jit(solution)/shard_map/block/pallas_call | solution.py:195
  129.7 1.3 collective-permute-start.14
  131.0 5.2 %grad.3 = (bf16[1,1536,256]{2,1,0:T(8,128)(2,1)}, bf16[1,1536,256]{2,1,0:T(8,128)(2,1)}) custom-call(s32[1]{0:T(128)} %bitcast.me_ref, bf16[1536,1024]{1,0:T(8,128)(2,1)} %get-tuple-element.127.refs_0_.refs_1_, bf16[4,3,1024,256]{3,2,1,0:T(8,128)(2,1)} %get-tuple-element.125.refs_1_.refs_2_.refs_3_, ...), custom_call_target="tpu_custom_call" | custom-call | flops 1000 | bytes 1000 | tf_op jit(solution)/shard_map/grad/pallas_call | solution.py:237
  136.2 7.0 %grad.4 = (bf16[2,1536,256]{2,1,0:T(8,128)(2,1)}, bf16[2,1536,256]{2,1,0:T(8,128)(2,1)}) custom-call(s32[1]{0:T(128)} %bitcast.me_ref, bf16[1536,1024]{1,0:T(8,128)(2,1)} %get-tuple-element.133.refs_0_, bf16[4,3,1024,256]{3,2,1,0:T(8,128)(2,1)} %get-tuple-element.125.refs_1_.refs_2_.refs_3_, bf16[4,3,1024,256]{3,2,1,0:T(8,128)(2,1)} %get-tuple-element.125.refs_1_.refs_2_.refs_3_), custom_call_target="tpu_custom_call" | custom-call | flops 1000 | bytes 1000 | tf_op jit(solution)/shard_map/grad/pallas_call | solution.py:237
  143.2 0.5 collective-permute-start.19
  143.7 3.5 %collective-permute-done.14 = bf16[264,1536]{1,0:T(8,128)(2,1)S(1)} collective-permute-done((bf16[264,1536]{1,0:T(8,128)(2,1)}, bf16[264,1536]{1,0:T(8,128)(2,1)S(1)}, u32[]{:S(2)}, u32[]{:S(2)}) %collective-permute-start.14) | collective-permute-done | bytes 811040 | tf_op jit(solution)/shard_map/ppermute | solution.py:22
  147.2 0.2 add_convert_fusion.5
  147.5 0.2 add_convert_fusion.4
  147.7 1.6 collective-permute-start.16
  149.3 1.4 collective-permute-start.17
  150.8 1.5 collective-permute-start.18
  152.2 9.5 %grad.5 = (bf16[3,1536,256]{2,1,0:T(8,128)(2,1)}, bf16[3,1536,256]{2,1,0:T(8,128)(2,1)}) custom-call(s32[1]{0:T(128)} %bitcast.me_ref, bf16[1536,1024]{1,0:T(8,128)(2,1)} %get-tuple-element.133.refs_0_, bf16[1536,1024]{1,0:T(8,128)(2,1)} %get-tuple-element.127.refs_0_.refs_1_, bf16[4,3,1024,256]{3,2,1,0:T(8,128)(2,1)} %get-tuple-element.125.refs_1_.refs_2_.refs_3_, ...), custom_call_target="tpu_custom_call" | custom-call | flops 1000 | bytes 1000 | tf_op jit(solution)/shard_map/grad/pallas_call | solution.py:237
  161.8 0.4 add_convert_fusion.1
  162.1 4.2 %collective-permute-done.18.refs_1_ = bf16[1,1536,256]{2,1,0:T(8,128)(2,1)S(1)} collective-permute-done((bf16[1,1536,256]{2,1,0:T(8,128)(2,1)S(1)}, bf16[1,1536,256]{2,1,0:T(8,128)(2,1)S(1)}, u32[]{:S(2)}, u32[]{:S(2)}) %collective-permute-start.18) | collective-permute-done | bytes 786464 | tf_op jit(solution)/shard_map/ppermute | solution.py:22
  166.4 0.2 collective-permute-done.17
  166.6 0.3 add_convert_fusion.3
  166.9 0.8 copy-done.14
  167.7 0.2 add_convert_fusion.2
  168.0 1.1 collective-permute-start.20
  169.1 0.5 collective-permute-start.22
  169.6 2.6 %collective-permute-start.23 = (bf16[264,1536]{1,0:T(8,128)(2,1)S(1)}, bf16[264,1536]{1,0:T(8,128)(2,1)S(1)}, u32[]{:S(2)}, u32[]{:S(2)}) collective-permute-start(bf16[264,1536]{1,0:T(8,128)(2,1)S(1)} %add_convert_fusion.3), channel_id=1, source_target_pairs={{0,4},{1,5},{2,6},{3,7},{4,0},{5,1},{6,2},{7,3},{8,12},{9,13},{10,... | collective-permute-start | bytes 2433032 | tf_op jit(solution)/shard_map/ppermute | solution.py:22
  172.2 1.5 collective-permute-start.24
  173.7 0.5 add_convert_fusion.refs_0_
  174.2 2.1 %final.2 = f32[1,256,1536]{2,1,0:T(8,128)} custom-call(bf16[3,1536,256]{2,1,0:T(8,128)(2,1)S(1)} %add_convert_fusion.refs_0_, bf16[1,1536,256]{2,1,0:T(8,128)(2,1)S(1)} %collective-permute-done.18.refs_1_), custom_call_target="tpu_custom_call" | custom-call | flops 1000 | bytes 1000 | tf_op jit(solution)/shard_map/final/pallas_call | solution.py:267
  176.3 12.2 %collective-permute-done.20 = bf16[264,1536]{1,0:T(8,128)(2,1)S(1)} collective-permute-done((bf16[264,1536]{1,0:T(8,128)(2,1)S(1)}, bf16[264,1536]{1,0:T(8,128)(2,1)S(1)}, u32[]{:S(2)}, u32[]{:S(2)}) %collective-permute-start.20) | collective-permute-done | bytes 811040 | tf_op jit(solution)/shard_map/ppermute | solution.py:22
  188.5 18.2 %collective-permute-done.22 = bf16[264,1536]{1,0:T(8,128)(2,1)S(1)} collective-permute-done((bf16[264,1536]{1,0:T(8,128)(2,1)S(1)}, bf16[264,1536]{1,0:T(8,128)(2,1)S(1)}, u32[]{:S(2)}, u32[]{:S(2)}) %collective-permute-start.22) | collective-permute-done | bytes 811040 | tf_op jit(solution)/shard_map/ppermute | solution.py:22
  206.7 0.4 fusion.3
  207.1 0.6 slice_bitcast_fusion.2
  207.7 0.9 fusion.4
  208.6 2.2 %final.3 = (f32[1,1536,256]{2,1,0:T(8,128)}, f32[1,1536,256]{2,1,0:T(8,128)}) custom-call(bf16[3,1536,256]{2,1,0:T(8,128)(2,1)S(1)} %add_convert_fusion.refs_0_, bf16[2,1536,256]{2,1,0:T(8,128)(2,1)S(1)} %collective-permute-done.24.refs_1_), custom_call_target="tpu_custom_call" | custom-call | flops 1000 | bytes 1000 | tf_op jit(solution)/shard_map/final/pallas_call | solution.py:267
  (62 shorter events, 0.5 us)
Async XLA Ops:
  0.6 2.9 %copy-start.21 = (bf16[128,1536]{1,0:T(8,128)(2,1)S(1)}, bf16[128,1536]{1,0:T(8,128)(2,1)}, u32[]{:S(2)}) copy-start(bf16[128,1536]{1,0:T(8,128)(2,1)} %param.10) | copy-start | bytes 1179652
  0.6 2.9 %copy-start.22 = (bf16[128,1536]{1,0:T(8,128)(2,1)S(1)}, bf16[128,1536]{1,0:T(8,128)(2,1)}, u32[]{:S(2)}) copy-start(bf16[128,1536]{1,0:T(8,128)(2,1)} %param.7) | copy-start | bytes 1179652
  3.5 1.4 copy-start.19
  3.5 1.8 copy-start.20
  3.6 9.3 %copy-start.4 = (bf16[264,1536]{1,0:T(8,128)(2,1)}, bf16[264,1536]{1,0:T(8,128)(2,1)S(1)}, u32[]{:S(2)}) copy-start(bf16[264,1536]{1,0:T(8,128)(2,1)S(1)} %fusion.1.refs_0_) | copy-start | bytes 2433028
  3.7 4.9 %copy-start.2 = (bf16[1,768,256]{2,1,0:T(8,128)(2,1)}, bf16[1,768,256]{2,1,0:T(8,128)(2,1)S(1)}, u32[]{:S(2)}) copy-start(bf16[1,768,256]{2,1,0:T(8,128)(2,1)S(1)} %get-tuple-element.89.refs_3_) | copy-start | bytes 1179652
  5.5 23.7 %copy-start = (bf16[5,768,256]{2,1,0:T(8,128)(2,1)}, bf16[5,768,256]{2,1,0:T(8,128)(2,1)S(1)}, u32[]{:S(2)}) copy-start(bf16[5,768,256]{2,1,0:T(8,128)(2,1)S(1)} %pad_maximum_fusion.refs_2_) | copy-start | bytes 5898244
  5.5 23.7 %collective-permute-start.4 = (bf16[5,768,256]{2,1,0:T(8,128)(2,1)S(1)}, bf16[5,768,256]{2,1,0:T(8,128)(2,1)}, u32[]{:S(2)}, u32[]{:S(2)}) collective-permute-start(bf16[5,768,256]{2,1,0:T(8,128)(2,1)S(1)} %pad_maximum_fusion.refs_2_), channel_id=1, source_target_pairs={{0,8},{8,0},{16,24},{24,16},{1,9},{9,1},{17,25},{25,17},{2,10},{10... | collective-permute-start | bytes 5898248 | tf_op jit(solution)/shard_map/ppermute | solution.py:22
  6.1 46.1 %collective-permute-start.2 = (bf16[5,768,256]{2,1,0:T(8,128)(2,1)S(1)}, bf16[5,768,256]{2,1,0:T(8,128)(2,1)}, u32[]{:S(2)}, u32[]{:S(2)}) collective-permute-start(bf16[5,768,256]{2,1,0:T(8,128)(2,1)S(1)} %pad_maximum_fusion.refs_2_), channel_id=1, source_target_pairs={{0,16},{8,24},{16,0},{24,8},{1,17},{9,25},{17,1},{25,9},{2,18},{10... | collective-permute-start | bytes 5898248 | tf_op jit(solution)/shard_map/ppermute | solution.py:22
  8.6 4.3 %collective-permute-start.5 = (bf16[1,768,256]{2,1,0:T(8,128)(2,1)S(1)}, bf16[1,768,256]{2,1,0:T(8,128)(2,1)S(1)}, u32[]{:S(2)}, u32[]{:S(2)}) collective-permute-start(bf16[1,768,256]{2,1,0:T(8,128)(2,1)S(1)} %get-tuple-element.89.refs_3_), channel_id=1, source_target_pairs={{0,8},{8,0},{16,24},{24,16},{1,9},{9,1},{17,25},{25,17},{2,10},{10... | collective-permute-start | bytes 1179656 | tf_op jit(solution)/shard_map/ppermute | solution.py:22
  8.8 20.4 %collective-permute-start.3 = (bf16[264,1536]{1,0:T(8,128)(2,1)S(1)}, bf16[264,1536]{1,0:T(8,128)(2,1)}, u32[]{:S(2)}, u32[]{:S(2)}) collective-permute-start(bf16[264,1536]{1,0:T(8,128)(2,1)S(1)} %fusion.1.refs_0_), channel_id=1, source_target_pairs={{0,1},{1,0},{2,3},{3,2},{4,5},{5,4},{6,7},{7,6},{8,9},{9,8},{10,11... | collective-permute-start | bytes 2433032 | tf_op jit(solution)/shard_map/ppermute | solution.py:22
  10.3 38.5 %collective-permute-start.1 = (bf16[264,1536]{1,0:T(8,128)(2,1)S(1)}, bf16[264,1536]{1,0:T(8,128)(2,1)}, u32[]{:S(2)}, u32[]{:S(2)}) collective-permute-start(bf16[264,1536]{1,0:T(8,128)(2,1)S(1)} %fusion.1.refs_0_), channel_id=1, source_target_pairs={{0,4},{1,5},{2,6},{3,7},{4,0},{5,1},{6,2},{7,3},{8,12},{9,13},{10,... | collective-permute-start | bytes 2433032 | tf_op jit(solution)/shard_map/ppermute | solution.py:22
  12.9 1.6 copy-start.5
  12.9 36.2 %collective-permute-start = (bf16[264,1536]{1,0:T(8,128)(2,1)S(1)}, bf16[264,1536]{1,0:T(8,128)(2,1)}, u32[]{:S(2)}, u32[]{:S(2)}) collective-permute-start(bf16[264,1536]{1,0:T(8,128)(2,1)S(1)} %fusion.1.refs_0_), channel_id=1, source_target_pairs={{0,2},{1,3},{2,0},{3,1},{4,6},{5,7},{6,4},{7,5},{8,10},{9,11},{10,... | collective-permute-start | bytes 2433032 | tf_op jit(solution)/shard_map/ppermute | solution.py:22
  29.2 26.3 %copy-start.3 = (bf16[1,768,256]{2,1,0:T(8,128)(2,1)S(1)}, bf16[1,768,256]{2,1,0:T(8,128)(2,1)}, u32[]{:S(2)}) copy-start(bf16[1,768,256]{2,1,0:T(8,128)(2,1)} %copy-done.2) | copy-start | bytes 1179652
  52.2 22.2 %collective-permute-start.9 = (bf16[5,768,256]{2,1,0:T(8,128)(2,1)}, bf16[5,768,256]{2,1,0:T(8,128)(2,1)S(1)}, u32[]{:S(2)}, u32[]{:S(2)}) collective-permute-start(bf16[5,768,256]{2,1,0:T(8,128)(2,1)} %collective-permute-done.2.refs_4_.refs_6_), channel_id=1, source_target_pairs={{0,8},{8,0},{16,24},{24,16},{1,9},{9,1},{17,25},{25,17},{2,10},{10... | collective-permute-start | bytes 5898248 | tf_op jit(solution)/shard_map/ppermute | solution.py:22
  52.2 20.7 %collective-permute-start.7 = (bf16[264,1536]{1,0:T(8,128)(2,1)}, bf16[264,1536]{1,0:T(8,128)(2,1)S(1)}, u32[]{:S(2)}, u32[]{:S(2)}) collective-permute-start(bf16[264,1536]{1,0:T(8,128)(2,1)} %collective-permute-done.refs_0_.refs_2_), channel_id=1, source_target_pairs={{0,1},{1,0},{2,3},{3,2},{4,5},{5,4},{6,7},{7,6},{8,9},{9,8},{10,11... | collective-permute-start | bytes 2433032 | tf_op jit(solution)/shard_map/ppermute | solution.py:22
  53.9 20.4 %collective-permute-start.6 = (bf16[264,1536]{1,0:T(8,128)(2,1)}, bf16[264,1536]{1,0:T(8,128)(2,1)S(1)}, u32[]{:S(2)}, u32[]{:S(2)}) collective-permute-start(bf16[264,1536]{1,0:T(8,128)(2,1)} %collective-permute-done.1.refs_1_.refs_3_), channel_id=1, source_target_pairs={{0,2},{1,3},{2,0},{3,1},{4,6},{5,7},{6,4},{7,5},{8,10},{9,11},{10,... | collective-permute-start | bytes 2433032 | tf_op jit(solution)/shard_map/ppermute | solution.py:22
  55.5 11.0 %collective-permute-start.8 = (bf16[1,768,256]{2,1,0:T(8,128)(2,1)S(1)}, bf16[1,768,256]{2,1,0:T(8,128)(2,1)S(1)}, u32[]{:S(2)}, u32[]{:S(2)}) collective-permute-start(bf16[1,768,256]{2,1,0:T(8,128)(2,1)S(1)} %copy-done.3), channel_id=1, source_target_pairs={{0,16},{8,24},{16,0},{24,8},{1,17},{9,25},{17,1},{25,9},{2,18},{10... | collective-permute-start | bytes 1179656 | tf_op jit(solution)/shard_map/ppermute | solution.py:22
  66.5 10.0 %copy-start.6 = (bf16[1,768,256]{2,1,0:T(8,128)(2,1)}, bf16[1,768,256]{2,1,0:T(8,128)(2,1)S(1)}, u32[]{:S(2)}) copy-start(bf16[1,768,256]{2,1,0:T(8,128)(2,1)S(1)} %collective-permute-done.8.refs_5_.refs_7_) | copy-start | bytes 1179652
  72.9 18.9 %copy-start.10 = (bf16[264,1536]{1,0:T(8,128)(2,1)}, bf16[264,1536]{1,0:T(8,128)(2,1)S(1)}, u32[]{:S(2)}) copy-start(bf16[264,1536]{1,0:T(8,128)(2,1)S(1)} %collective-permute-done.7.refs_0_) | copy-start | bytes 2433028
  74.4 17.4 %copy-start.11 = (bf16[264,1536]{1,0:T(8,128)(2,1)}, bf16[264,1536]{1,0:T(8,128)(2,1)S(1)}, u32[]{:S(2)}) copy-start(bf16[264,1536]{1,0:T(8,128)(2,1)S(1)} %collective-permute-done.6.refs_0_) | copy-start | bytes 2433028
  74.4 2.1 %copy-start.1 = (bf16[5,768,256]{2,1,0:T(8,128)(2,1)}, bf16[5,768,256]{2,1,0:T(8,128)(2,1)S(1)}, u32[]{:S(2)}) copy-start(bf16[5,768,256]{2,1,0:T(8,128)(2,1)S(1)} %collective-permute-done.9.refs_6_.refs_8_) | copy-start | bytes 5898244
  74.4 19.4 %collective-permute-start.11 = (bf16[264,1536]{1,0:T(8,128)(2,1)S(1)}, bf16[264,1536]{1,0:T(8,128)(2,1)S(1)}, u32[]{:S(2)}, u32[]{:S(2)}) collective-permute-start(bf16[264,1536]{1,0:T(8,128)(2,1)S(1)} %collective-permute-done.6.refs_0_), channel_id=1, source_target_pairs={{0,1},{1,0},{2,3},{3,2},{4,5},{5,4},{6,7},{7,6},{8,9},{9,8},{10,11... | collective-permute-start | bytes 2433032 | tf_op jit(solution)/shard_map/ppermute | solution.py:22
  74.8 1.7 collective-permute-start.10
  76.5 0.7 copy-start.7
  93.8 0.9 copy-start.12
  93.8 20.6 %collective-permute-start.12 = (bf16[264,1536]{1,0:T(8,128)(2,1)}, bf16[264,1536]{1,0:T(8,128)(2,1)S(1)}, u32[]{:S(2)}, u32[]{:S(2)}) collective-permute-start(bf16[264,1536]{1,0:T(8,128)(2,1)} %collective-permute-done.1.refs_1_.refs_3_), channel_id=1, source_target_pairs={{0,1},{1,0},{2,3},{3,2},{4,5},{5,4},{6,7},{7,6},{8,9},{9,8},{10,11... | collective-permute-start | bytes 2433032 | tf_op jit(solution)/shard_map/ppermute | solution.py:22
  108.8 34.8 %collective-permute-start.15 = (bf16[264,1536]{1,0:T(8,128)(2,1)}, bf16[264,1536]{1,0:T(8,128)(2,1)S(1)}, u32[]{:S(2)}, u32[]{:S(2)}) collective-permute-start(bf16[264,1536]{1,0:T(8,128)(2,1)} %get-tuple-element.130), channel_id=1, source_target_pairs={{0,1},{1,0},{2,3},{3,2},{4,5},{5,4},{6,7},{7,6},{8,9},{9,8},{10,11... | collective-permute-start | bytes 2433032 | tf_op jit(solution)/shard_map/ppermute | solution.py:22
  114.4 0.9 copy-start.13
  129.7 17.5 %collective-permute-start.14 = (bf16[264,1536]{1,0:T(8,128)(2,1)}, bf16[264,1536]{1,0:T(8,128)(2,1)S(1)}, u32[]{:S(2)}, u32[]{:S(2)}) collective-permute-start(bf16[264,1536]{1,0:T(8,128)(2,1)} %get-tuple-element.129), channel_id=1, source_target_pairs={{0,1},{1,0},{2,3},{3,2},{4,5},{5,4},{6,7},{7,6},{8,9},{9,8},{10,11... | collective-permute-start | bytes 2433032 | tf_op jit(solution)/shard_map/ppermute | solution.py:22
  136.2 7.5 %collective-permute-start.13 = (bf16[1,1536,256]{2,1,0:T(8,128)(2,1)}, bf16[1,1536,256]{2,1,0:T(8,128)(2,1)S(1)}, u32[]{:S(2)}, u32[]{:S(2)}) collective-permute-start(bf16[1,1536,256]{2,1,0:T(8,128)(2,1)} %get-tuple-element.128), channel_id=1, source_target_pairs={{0,8},{8,0},{16,24},{24,16},{1,9},{9,1},{17,25},{25,17},{2,10},{10... | collective-permute-start | bytes 2359304 | tf_op jit(solution)/shard_map/ppermute | solution.py:22
  136.2 11.1 %copy-start.18 = (bf16[1,1536,256]{2,1,0:T(8,128)(2,1)S(1)}, bf16[1,1536,256]{2,1,0:T(8,128)(2,1)}, u32[]{:S(2)}) copy-start(bf16[1,1536,256]{2,1,0:T(8,128)(2,1)} %get-tuple-element.131) | copy-start | bytes 2359300
  143.2 4.3 %copy-start.16 = (bf16[264,1536]{1,0:T(8,128)(2,1)S(1)}, bf16[264,1536]{1,0:T(8,128)(2,1)}, u32[]{:S(2)}) copy-start(bf16[264,1536]{1,0:T(8,128)(2,1)} %get-tuple-element.118) | copy-start | bytes 2433028
  143.2 18.5 %collective-permute-start.19 = (bf16[2,1536,256]{2,1,0:T(8,128)(2,1)}, bf16[2,1536,256]{2,1,0:T(8,128)(2,1)S(1)}, u32[]{:S(2)}, u32[]{:S(2)}) collective-permute-start(bf16[2,1536,256]{2,1,0:T(8,128)(2,1)} %get-tuple-element.135), channel_id=1, source_target_pairs={{0,8},{8,0},{16,24},{24,16},{1,9},{9,1},{17,25},{25,17},{2,10},{10... | collective-permute-start | bytes 4718600 | tf_op jit(solution)/shard_map/ppermute | solution.py:22
  147.7 14.1 %copy-start.9 = (bf16[2,1536,256]{2,1,0:T(8,128)(2,1)S(1)}, bf16[2,1536,256]{2,1,0:T(8,128)(2,1)}, u32[]{:S(2)}) copy-start(bf16[2,1536,256]{2,1,0:T(8,128)(2,1)} %get-tuple-element.134) | copy-start | bytes 4718596
  147.7 18.7 %collective-permute-start.16 = (bf16[264,1536]{1,0:T(8,128)(2,1)S(1)}, bf16[264,1536]{1,0:T(8,128)(2,1)S(1)}, u32[]{:S(2)}, u32[]{:S(2)}) collective-permute-start(bf16[264,1536]{1,0:T(8,128)(2,1)S(1)} %add_convert_fusion.4), channel_id=1, source_target_pairs={{0,2},{1,3},{2,0},{3,1},{4,6},{5,7},{6,4},{7,5},{8,10},{9,11},{10,... | collective-permute-start | bytes 2433032 | tf_op jit(solution)/shard_map/ppermute | solution.py:22
  149.3 17.3 %collective-permute-start.17 = (bf16[264,1536]{1,0:T(8,128)(2,1)}, bf16[264,1536]{1,0:T(8,128)(2,1)S(1)}, u32[]{:S(2)}, u32[]{:S(2)}) collective-permute-start(bf16[264,1536]{1,0:T(8,128)(2,1)} %get-tuple-element.141), channel_id=1, source_target_pairs={{0,1},{1,0},{2,3},{3,2},{4,5},{5,4},{6,7},{7,6},{8,9},{9,8},{10,11... | collective-permute-start | bytes 2433032 | tf_op jit(solution)/shard_map/ppermute | solution.py:22
  150.8 15.6 %collective-permute-start.18 = (bf16[1,1536,256]{2,1,0:T(8,128)(2,1)S(1)}, bf16[1,1536,256]{2,1,0:T(8,128)(2,1)S(1)}, u32[]{:S(2)}, u32[]{:S(2)}) collective-permute-start(bf16[1,1536,256]{2,1,0:T(8,128)(2,1)S(1)} %add_convert_fusion.5), channel_id=1, source_target_pairs={{0,16},{8,24},{16,0},{24,8},{1,17},{9,25},{17,1},{25,9},{2,18},{10... | collective-permute-start | bytes 2359304 | tf_op jit(solution)/shard_map/ppermute | solution.py:22
  161.7 4.9 %copy-start.23 = (bf16[3,1536,256]{2,1,0:T(8,128)(2,1)S(1)}, bf16[3,1536,256]{2,1,0:T(8,128)(2,1)}, u32[]{:S(2)}) copy-start(bf16[3,1536,256]{2,1,0:T(8,128)(2,1)} %get-tuple-element.152) | copy-start | bytes 7077892
  161.8 4.8 %copy-start.15 = (bf16[264,1536]{1,0:T(8,128)(2,1)S(1)}, bf16[264,1536]{1,0:T(8,128)(2,1)}, u32[]{:S(2)}) copy-start(bf16[264,1536]{1,0:T(8,128)(2,1)} %get-tuple-element.147) | copy-start | bytes 2433028
  166.6 7.1 %collective-permute-start.21 = (bf16[3,1536,256]{2,1,0:T(8,128)(2,1)S(1)}, bf16[3,1536,256]{2,1,0:T(8,128)(2,1)S(1)}, u32[]{:S(2)}, u32[]{:S(2)}) collective-permute-start(bf16[3,1536,256]{2,1,0:T(8,128)(2,1)S(1)} %copy-done.23), channel_id=1, source_target_pairs={{0,8},{8,0},{16,24},{24,16},{1,9},{9,1},{17,25},{25,17},{2,10},{10... | collective-permute-start | bytes 7077896 | tf_op jit(solution)/shard_map/ppermute | solution.py:22
  166.6 1.1 copy-start.14
  166.6 1.4 copy-start.24
  166.9 6.7 %copy-start.8 = (bf16[3,1536,256]{2,1,0:T(8,128)(2,1)S(1)}, bf16[3,1536,256]{2,1,0:T(8,128)(2,1)}, u32[]{:S(2)}) copy-start(bf16[3,1536,256]{2,1,0:T(8,128)(2,1)} %get-tuple-element.151) | copy-start | bytes 7077892
  168.0 20.5 %collective-permute-start.20 = (bf16[264,1536]{1,0:T(8,128)(2,1)S(1)}, bf16[264,1536]{1,0:T(8,128)(2,1)S(1)}, u32[]{:S(2)}, u32[]{:S(2)}) collective-permute-start(bf16[264,1536]{1,0:T(8,128)(2,1)S(1)} %copy-done.24), channel_id=1, source_target_pairs={{0,1},{1,0},{2,3},{3,2},{4,5},{5,4},{6,7},{7,6},{8,9},{9,8},{10,11... | collective-permute-start | bytes 2433032 | tf_op jit(solution)/shard_map/ppermute | solution.py:22
  169.1 37.6 %collective-permute-start.22 = (bf16[264,1536]{1,0:T(8,128)(2,1)S(1)}, bf16[264,1536]{1,0:T(8,128)(2,1)S(1)}, u32[]{:S(2)}, u32[]{:S(2)}) collective-permute-start(bf16[264,1536]{1,0:T(8,128)(2,1)S(1)} %add_convert_fusion.2), channel_id=1, source_target_pairs={{0,2},{1,3},{2,0},{3,1},{4,6},{5,7},{6,4},{7,5},{8,10},{9,11},{10,... | collective-permute-start | bytes 2433032 | tf_op jit(solution)/shard_map/ppermute | solution.py:22
  169.6 37.1 %collective-permute-start.23 = (bf16[264,1536]{1,0:T(8,128)(2,1)S(1)}, bf16[264,1536]{1,0:T(8,128)(2,1)S(1)}, u32[]{:S(2)}, u32[]{:S(2)}) collective-permute-start(bf16[264,1536]{1,0:T(8,128)(2,1)S(1)} %add_convert_fusion.3), channel_id=1, source_target_pairs={{0,4},{1,5},{2,6},{3,7},{4,0},{5,1},{6,2},{7,3},{8,12},{9,13},{10,... | collective-permute-start | bytes 2433032 | tf_op jit(solution)/shard_map/ppermute | solution.py:22
  172.2 36.5 %collective-permute-start.24 = (bf16[2,1536,256]{2,1,0:T(8,128)(2,1)S(1)}, bf16[2,1536,256]{2,1,0:T(8,128)(2,1)S(1)}, u32[]{:S(2)}, u32[]{:S(2)}) collective-permute-start(bf16[2,1536,256]{2,1,0:T(8,128)(2,1)S(1)} %add_convert_fusion.1), channel_id=1, source_target_pairs={{0,16},{8,24},{16,0},{24,8},{1,17},{9,25},{17,1},{25,9},{2,18},{10... | collective-permute-start | bytes 4718600 | tf_op jit(solution)/shard_map/ppermute | solution.py:22
  174.2 32.5 %copy-start.17 = (bf16[264,1536]{1,0:T(8,128)(2,1)S(1)}, bf16[264,1536]{1,0:T(8,128)(2,1)}, u32[]{:S(2)}) copy-start(bf16[264,1536]{1,0:T(8,128)(2,1)} %get-tuple-element.105) | copy-start | bytes 2433028
